TPU v7x, 32 devices: a whole 2x2x4 slice. The times are simulated.
32 devices in a mesh: fsdp: 16 (over z, x, core), seq: 2 (over y).
Axes of the slice: x: 2, y: 2, z: 4, core: 2. Of those that a mesh axis runs over, the one named last changes fastest.
Arguments:
- inputs: bfloat16 [32, 1024, 896], P('fsdp', 'seq'), may hold values from -6 to 6
- positions: int32 [32, 1024], P('fsdp', 'seq'), may hold values from 0 to 8188, as said below
- qkv_weight: bfloat16 [896, 1152], P('fsdp'), may hold values from -0.1875 to 0.1875
- qkv_bias: bfloat16 [1152], P('fsdp'), may hold values from -3 to 3
- output_weight: bfloat16 [896, 896], P('fsdp'), may hold values from -1 to 1
- first_gain: bfloat16 [896], P('fsdp'), may hold values from 0.25 to 1.75
- gate_weight: bfloat16 [896, 4864], P('fsdp'), may hold values from -0.1875 to 0.1875
- up_weight: bfloat16 [896, 4864], P('fsdp'), may hold values from -0.1875 to 0.1875
- down_weight: bfloat16 [4864, 896], P('fsdp'), may hold values from -0.15625 to 0.15625
- second_gain: bfloat16 [896], P('fsdp'), may hold values from 0.25 to 1.75
- cotangent: bfloat16 [32, 1024, 896], P('fsdp', 'seq'), may hold values from -6 to 6
Outputs:
- result: bfloat16 [32, 1024, 896], P('fsdp', 'seq')
- input_grad: float32 [32, 1024, 896], P('fsdp', 'seq')
- qkv_grad: float32 [896, 1152], P(('fsdp', 'seq'))
- bias_grad: float32 [1152], P(('fsdp', 'seq'))
- output_grad: float32 [896, 896], P(('fsdp', 'seq'))
- first_grad: float32 [896], P(('fsdp', 'seq'))
- gate_grad: float32 [896, 4864], P(('fsdp', 'seq'))
- up_grad: float32 [896, 4864], P(('fsdp', 'seq'))
- down_grad: float32 [4864, 896], P(('fsdp', 'seq'))
- second_grad: float32 [896], P(('fsdp', 'seq'))
Inputs may be any that keep to these rules, and one draw needn't show every extreme that they name: Along each sequence the positions rise strictly, by 1 to 4 from one token to the next, from a first position between 0 and 4096; some sequence begins at 0, and some sequence begins at 4096 and rises by 4 at every token.
All inputs are finite; a program needn't handle non-finite values.
Results may differ from a plain program's by a relative error of at most 0.015.
Values may be sent and summed in bfloat16 or wider, within the bound.
A program may use at most 320 MiB of HBM per device.

v0:
```python
import jax
import jax.numpy as jnp
from jax import lax
from jax.sharding import PartitionSpec as P

HEADS = 14
KV_HEADS = 2
HEAD_DIM = 64
QBLOCK = 512


EPS = 1e-06
THETA = 1000000.0


def rms_norm(values, gain):
    scale = lax.rsqrt(jnp.mean(values * values, axis=-1, keepdims=True) + EPS)
    return (values * scale * gain, scale)


def rms_back(values, scale, gain, upstream):
    weighted = upstream * gain
    inner = jnp.mean(weighted * values, axis=-1, keepdims=True)
    grad_in = scale * weighted - values * (scale * scale * scale) * inner
    grad_gain = jnp.sum(upstream * values * scale, axis=(0, 1))
    return (grad_in, grad_gain)


def rope_tables(positions):
    freqs = THETA ** (-jnp.arange(0, HEAD_DIM, 2).astype(jnp.float32) / HEAD_DIM)
    angles = positions.astype(jnp.float32)[..., None] * freqs
    angles = jnp.concatenate([angles, angles], axis=-1)
    return (jnp.cos(angles), jnp.sin(angles))


def rotate(values, cosine, sine):
    half = HEAD_DIM // 2
    turned = jnp.concatenate([-values[..., half:], values[..., :half]], axis=-1)
    return values * cosine + turned * sine


def rotate_back(grads, cosine, sine):
    half = HEAD_DIM // 2
    scaled = grads * sine
    turned = jnp.concatenate([scaled[..., half:], -scaled[..., :half]], axis=-1)
    return grads * cosine + turned


def masked_scores(rows, key_full, start, scale):
    scores = (
        jnp.einsum("sicgd,sjcd->scgij", rows, key_full, preferred_element_type=jnp.float32) * scale
    )
    row_index = start + lax.iota(jnp.int32, rows.shape[1])
    col_index = lax.iota(jnp.int32, key_full.shape[1])
    allowed = row_index[:, None] >= col_index[None, :]
    return jnp.where(allowed, scores, -1e30)


def shards(
    inputs,
    positions,
    qkv_weight,
    qkv_bias,
    output_weight,
    first_gain,
    gate_weight,
    up_weight,
    down_weight,
    second_gain,
    cotangent,
):
    seqs, half_len, width = inputs.shape
    nseq = lax.axis_size("seq")
    length = half_len * nseq
    qwidth = HEADS * HEAD_DIM
    kvwidth = KV_HEADS * HEAD_DIM
    local_kv = KV_HEADS // nseq
    local_heads = HEADS // nseq
    group = HEADS // KV_HEADS
    nblocks = length // QBLOCK
    scale = HEAD_DIM ** (-0.5)
    full_qkv, full_bias, full_output, full_gain1 = (
        lax.all_gather(qkv_weight, "fsdp", axis=0, tiled=True),
        lax.all_gather(qkv_bias, "fsdp", axis=0, tiled=True),
        lax.all_gather(output_weight, "fsdp", axis=0, tiled=True),
        lax.all_gather(first_gain, "fsdp", axis=0, tiled=True),
    )
    full_gate, full_up, full_down, full_gain2 = (
        lax.all_gather(gate_weight, "fsdp", axis=0, tiled=True),
        lax.all_gather(up_weight, "fsdp", axis=0, tiled=True),
        lax.all_gather(down_weight, "fsdp", axis=0, tiled=True),
        lax.all_gather(second_gain, "fsdp", axis=0, tiled=True),
    )
    tokens = inputs.astype(jnp.float32)
    gain1 = full_gain1.astype(jnp.float32)
    normed1, scale1 = rms_norm(tokens, gain1)
    normed1_low = normed1.astype(jnp.bfloat16)
    pre = jnp.dot(normed1_low, full_qkv, preferred_element_type=jnp.float32) + full_bias.astype(
        jnp.float32
    )
    cosine, sine = rope_tables(positions)
    cosine = cosine[:, :, None, :]
    sine = sine[:, :, None, :]
    query = pre[..., :qwidth].reshape(seqs, half_len, HEADS, HEAD_DIM)
    keys = pre[..., qwidth : qwidth + kvwidth].reshape(seqs, half_len, KV_HEADS, HEAD_DIM)
    values = pre[..., qwidth + kvwidth :].reshape(seqs, half_len, KV_HEADS, HEAD_DIM)
    query_low = rotate(query, cosine, sine).astype(jnp.bfloat16)
    pair_low = jnp.concatenate([rotate(keys, cosine, sine), values], axis=-1).astype(jnp.bfloat16)
    query_heads, pair_heads = (
        lax.all_to_all(query_low, "seq", split_axis=2, concat_axis=1, tiled=True),
        lax.all_to_all(pair_low, "seq", split_axis=2, concat_axis=1, tiled=True),
    )
    query_five = query_heads.reshape(seqs, length, local_kv, group, HEAD_DIM)
    key_full = pair_heads[..., :HEAD_DIM]
    value_full = pair_heads[..., HEAD_DIM:]
    starts = jnp.arange(nblocks, dtype=jnp.int32) * QBLOCK

    def forward_block(start):
        rows = lax.dynamic_slice_in_dim(query_five, start, QBLOCK, 1)
        scores = masked_scores(rows, key_full, start, scale)
        top = jnp.max(scores, axis=-1, keepdims=True)
        expo = jnp.exp(scores - top)
        total = jnp.sum(expo, axis=-1, keepdims=True)
        probs_low = (expo / total).astype(jnp.bfloat16)
        mixed = jnp.einsum(
            "scgij,sjcd->sicgd", probs_low, value_full, preferred_element_type=jnp.float32
        )
        return (mixed.astype(jnp.bfloat16), (top + jnp.log(total))[..., 0])

    mixed_blocks, log_totals = lax.map(forward_block, starts)
    mixed_heads = jnp.moveaxis(mixed_blocks, 0, 1).reshape(seqs, length, local_heads, HEAD_DIM)
    mixed_tokens = lax.all_to_all(
        mixed_heads, "seq", split_axis=1, concat_axis=2, tiled=True
    ).reshape(seqs, half_len, qwidth)
    hidden = tokens + jnp.dot(mixed_tokens, full_output, preferred_element_type=jnp.float32)
    gain2 = full_gain2.astype(jnp.float32)
    normed2, scale2 = rms_norm(hidden, gain2)
    normed2_low = normed2.astype(jnp.bfloat16)
    gate = jnp.dot(normed2_low, full_gate, preferred_element_type=jnp.float32)
    up = jnp.dot(normed2_low, full_up, preferred_element_type=jnp.float32)
    sigma = jax.nn.sigmoid(gate)
    silu = gate * sigma
    act_low = (silu * up).astype(jnp.bfloat16)
    result = (hidden + jnp.dot(act_low, full_down, preferred_element_type=jnp.float32)).astype(
        jnp.bfloat16
    )
    full_qkv, full_bias, full_output, full_gain1 = (
        lax.all_gather(qkv_weight, "fsdp", axis=0, tiled=True),
        lax.all_gather(qkv_bias, "fsdp", axis=0, tiled=True),
        lax.all_gather(output_weight, "fsdp", axis=0, tiled=True),
        lax.all_gather(first_gain, "fsdp", axis=0, tiled=True),
    )
    full_gate, full_up, full_down, full_gain2 = (
        lax.all_gather(gate_weight, "fsdp", axis=0, tiled=True),
        lax.all_gather(up_weight, "fsdp", axis=0, tiled=True),
        lax.all_gather(down_weight, "fsdp", axis=0, tiled=True),
        lax.all_gather(second_gain, "fsdp", axis=0, tiled=True),
    )
    grad_out = cotangent.astype(jnp.float32)
    down_grad = jnp.einsum("stf,std->fd", act_low, cotangent, preferred_element_type=jnp.float32)
    d_act = jnp.einsum("std,fd->stf", cotangent, full_down, preferred_element_type=jnp.float32)
    d_gate = (d_act * up * sigma * (1.0 + gate * (1.0 - sigma))).astype(jnp.bfloat16)
    d_up = (d_act * silu).astype(jnp.bfloat16)
    gate_grad = jnp.einsum("std,stf->df", normed2_low, d_gate, preferred_element_type=jnp.float32)
    up_grad = jnp.einsum("std,stf->df", normed2_low, d_up, preferred_element_type=jnp.float32)
    d_normed2 = jnp.einsum("stf,df->std", d_gate, full_gate, preferred_element_type=jnp.float32)
    d_normed2 = d_normed2 + jnp.einsum(
        "stf,df->std", d_up, full_up, preferred_element_type=jnp.float32
    )
    back2, second_grad = rms_back(hidden, scale2, gain2, d_normed2)
    d_hidden = grad_out + back2
    d_branch = d_hidden.astype(jnp.bfloat16)
    output_grad = jnp.einsum(
        "stq,std->qd", mixed_tokens, d_branch, preferred_element_type=jnp.float32
    )
    d_mixed = jnp.einsum("std,qd->stq", d_branch, full_output, preferred_element_type=jnp.float32)
    d_mixed = d_mixed.astype(jnp.bfloat16).reshape(seqs, half_len, HEADS, HEAD_DIM)
    d_heads = lax.all_to_all(d_mixed, "seq", split_axis=2, concat_axis=1, tiled=True)
    d_heads = d_heads.reshape(seqs, length, local_kv, group, HEAD_DIM)

    def backward_block(carry, item):
        start, log_total = item
        key_sum, value_sum = carry
        rows = lax.dynamic_slice_in_dim(query_five, start, QBLOCK, 1)
        grad_rows = lax.dynamic_slice_in_dim(d_heads, start, QBLOCK, 1)
        scores = masked_scores(rows, key_full, start, scale)
        probs = jnp.exp(scores - log_total[..., None])
        probs_low = probs.astype(jnp.bfloat16)
        d_probs = jnp.einsum(
            "sicgd,sjcd->scgij", grad_rows, value_full, preferred_element_type=jnp.float32
        )
        d_scores = probs * (d_probs - jnp.sum(probs * d_probs, axis=-1, keepdims=True))
        d_scores = d_scores.astype(jnp.bfloat16)
        d_rows = (
            jnp.einsum("scgij,sjcd->sicgd", d_scores, key_full, preferred_element_type=jnp.float32)
            * scale
        )
        key_sum = (
            key_sum
            + jnp.einsum("scgij,sicgd->sjcd", d_scores, rows, preferred_element_type=jnp.float32)
            * scale
        )
        value_sum = value_sum + jnp.einsum(
            "scgij,sicgd->sjcd", probs_low, grad_rows, preferred_element_type=jnp.float32
        )
        return ((key_sum, value_sum), d_rows.astype(jnp.bfloat16))

    zeros = jnp.zeros((seqs, length, local_kv, HEAD_DIM), jnp.float32)
    (key_sum, value_sum), d_query_blocks = lax.scan(
        backward_block, (zeros, zeros), (starts, log_totals)
    )
    d_query = jnp.moveaxis(d_query_blocks, 0, 1).reshape(seqs, length, local_heads, HEAD_DIM)
    d_pair = jnp.concatenate([key_sum, value_sum], axis=-1).astype(jnp.bfloat16)
    back_query, back_pair = (
        lax.all_to_all(d_query, "seq", split_axis=1, concat_axis=2, tiled=True),
        lax.all_to_all(d_pair, "seq", split_axis=1, concat_axis=2, tiled=True),
    )
    query_pre = rotate_back(back_query.astype(jnp.float32), cosine, sine).reshape(
        seqs, half_len, qwidth
    )
    key_pre = rotate_back(back_pair[..., :HEAD_DIM].astype(jnp.float32), cosine, sine).reshape(
        seqs, half_len, kvwidth
    )
    value_pre = back_pair[..., HEAD_DIM:].astype(jnp.float32).reshape(seqs, half_len, kvwidth)
    d_pre = jnp.concatenate([query_pre, key_pre, value_pre], axis=-1).astype(jnp.bfloat16)
    qkv_grad = jnp.einsum("std,stc->dc", normed1_low, d_pre, preferred_element_type=jnp.float32)
    bias_grad = jnp.sum(d_pre.astype(jnp.float32), axis=(0, 1))
    d_normed1 = jnp.einsum("stc,dc->std", d_pre, full_qkv, preferred_element_type=jnp.float32)
    back1, first_grad = rms_back(tokens, scale1, gain1, d_normed1)
    input_grad = d_hidden + back1
    qkv_part, bias_part, output_part, first_part, gate_part, up_part, down_part, second_part = (
        lax.psum_scatter(qkv_grad, ("fsdp", "seq"), scatter_dimension=0, tiled=True),
        lax.psum_scatter(bias_grad, ("fsdp", "seq"), scatter_dimension=0, tiled=True),
        lax.psum_scatter(output_grad, ("fsdp", "seq"), scatter_dimension=0, tiled=True),
        lax.psum_scatter(first_grad, ("fsdp", "seq"), scatter_dimension=0, tiled=True),
        lax.psum_scatter(gate_grad, ("fsdp", "seq"), scatter_dimension=0, tiled=True),
        lax.psum_scatter(up_grad, ("fsdp", "seq"), scatter_dimension=0, tiled=True),
        lax.psum_scatter(down_grad, ("fsdp", "seq"), scatter_dimension=0, tiled=True),
        lax.psum_scatter(second_grad, ("fsdp", "seq"), scatter_dimension=0, tiled=True),
    )
    return (
        result,
        input_grad,
        qkv_part,
        bias_part,
        output_part,
        first_part,
        gate_part,
        up_part,
        down_part,
        second_part,
    )


def solution(mesh):
    placed = (
        P("fsdp", "seq", None),
        P("fsdp", "seq"),
        P("fsdp", None),
        P("fsdp"),
        P("fsdp", None),
        P("fsdp"),
        P("fsdp", None),
        P("fsdp", None),
        P("fsdp", None),
        P("fsdp"),
        P("fsdp", "seq", None),
    )
    return jax.shard_map(
        shards,
        mesh=mesh,
        in_specs=placed,
        out_specs=(
            P("fsdp", "seq", None),
            P("fsdp", "seq", None),
            P(("fsdp", "seq"), None),
            P(("fsdp", "seq")),
            P(("fsdp", "seq"), None),
            P(("fsdp", "seq")),
            P(("fsdp", "seq"), None),
            P(("fsdp", "seq"), None),
            P(("fsdp", "seq"), None),
            P(("fsdp", "seq")),
        ),
        check_vma=False,
    )
```

profile of v0, /device:TPU:0, one launch (start us, length us, event | category | flops | bytes accessed | tf_op | source)
XLA Modules:
  0.0 2048.7 jit_solution(219067381755549266)
XLA Ops:
  15.1 36.4 %all-reduce.16 = (bf16[1152]{0:T(1024)(128)(2,1)S(1)}, bf16[896]{0:T(1024)(128)(2,1)S(1)}, bf16[896]{0:T(1024)(128)(2,1)}) all-reduce(bf16[1152]{0:T(1024)(128)(2,1)S(1)} %dynamic-update-slice.1, bf16[896]{0:T(1024)(128)(2,1)S(1)} %dynamic-update-slice, bf16[896]{0:T(1024)(128)(2,1)S(1)} %dynamic-update-slice.2), channel_id=1, replica_groups=mesh['fsdp'=16,'seq'=2] {'fsdp'}, use_global_device_ids=true, to_apply=%add.1 | all-reduce | flops 2944 | bytes 11776
  87.5 16.9 all-to-all-done
  107.5 5.6 reshape.273
  114.6 93.3 %while.27 = (s32[]{:T(128)}, bf16[2,2,512,1,7,64]{2,5,4,1,3,0:T(8,128)(2,1)}, f32[2,2,1,7,512]{4,3,1,2,0:T(8,128)}, s32[2]{0:T(128)S(1)}, bf16[2,1024,1,7,64]{1,...) while((s32[]{:T(128)}, ...), condition=%wide.region_4.5_spmd, body=%wide.region_1.4_spmd.sunk | while | flops 1968104960 | bytes 210215104 | solution.py:130
  118.1 14.9 fusion.146
  133.0 15.0 fusion.147
  151.1 9.7 fusion.148
  165.0 14.1 fusion.146
  179.1 15.1 fusion.147
  197.5 9.7 fusion.148
  207.9 9.8 copy.207
  234.0 12.5 all-to-all-done.2
  250.0 9.6 copy.169
  267.8 17.1 fusion.62
  284.8 18.5 fusion.68
  303.3 24.4 %all-gather.10.cloned.1.call-done = bf16[896,4864]{1,0:T(8,128)(2,1)} async-done(((bf16[56,4864]{1,0:T(8,128)(2,1)}), bf16[896,4864]{1,0:T(8,128)(2,1)}) %all-gather.10.cloned.1.call-update) | async-done | bytes 8716304 | tf_op jit(solution)/shard_map/all_gather | solution.py:89
  327.7 31.9 %multiply_convert_fusion.2 = (bf16[2,512,4864]{2,1,0:T(8,128)(2,1)}, bf16[2,512,4864]{2,1,0:T(8,128)(2,1)}, bf16[2,512,4864]{2,1,0:T(8,128)(2,1)}) fusion(f32[2,512,4864]{2,1,0:T(8,128)} %fusion.62, f32[2,512,4864]{2,1,0:T(8,128)} %fusion.68, bf16[2,512,896]{2,1,0:T(8,128)(2,1)S(1)} %copy-done.26, bf16[896,4864]{1,0:T(8,128)(2,1)} %all-gather.10.cloned.1.call-done), kind=kOutput, calls=%fused_computation.62 | convolution fusion | flops 9000189952 | bytes 80281600 | tf_op jit(solution)/shard_map/dot_general | solution.py:139
  359.6 17.0 fusion.66
  376.6 17.5 multiply_reduce_fusion
  409.8 17.4 convolution_bitcast_fusion.1
  427.2 16.3 convolution_bitcast_fusion.3
  452.9 192.0 %while.28 = (s32[]{:T(128)}, f32[2,1024,1,64]{1,3,0,2:T(8,128)S(1)}, f32[2,1024,1,64]{1,3,0,2:T(8,128)S(1)}, bf16[2,2,512,1,7,64]{2,5,4,1,3,0:T(8,128)(2,1)}, s3...) while((s32[]{:T(128)}, ...), condition=%wide.region_9.10_spmd.clone, body=%wide.region_7.9_spmd.clone.sunk | while | flops 4765771264 | bytes 228868304 | solution.py:209
  455.6 12.3 fusion.157
  468.9 23.8 %fusion.158 = (f32[2,7,512]{2,1,0:T(8,128)S(1)}, f32[2,1,7,512,1024]{4,3,2,0,1:T(8,128)}) fusion(f32[2,512,7,1024]{3,1,2,0:T(8,128)} %fusion.157, f32[2,7,512]{2,1,0:T(8,128)S(1)} %dynamic-slice_bitcast_fusion.2, bf16[2,1024,1,64]{1,3,0,2:T(8,128)(2,1)S(1)} %get-tuple-element.461, bf16[2,1024,1,7,64]{1,4,3,0,2:T(8,128)(2,1)} %get-tuple-element.460, ...), kind=kOutput, calls=%fused_computation.26.clone.1 | convolution fusion | flops 976217088 | bytes 60481540 | tf_op jit(solution)/shard_map/while/body/eval_jaxpr/sicgd,sjcd->scgij/dot_general | solution.py:51
  492.8 24.6 %fusion.159 = bf16[2,7,512,1024]{3,2,1,0:T(8,128)(2,1)} fusion(f32[2,1,7,512,1024]{4,3,2,0,1:T(8,128)} %get-tuple-element.397, f32[2,512,7,1024]{3,1,2,0:T(8,128)} %fusion.157, f32[2,7,512]{2,1,0:T(8,128)S(1)} %get-tuple-element.398), kind=kLoop, calls=%fused_computation.29.clone.1 | loop fusion | flops 22020096 | bytes 73428992 | tf_op jit(solution)/shard_map/reshape.31
  517.4 8.4 fusion.160
  525.8 12.3 fusion.161
  538.1 10.7 fusion.162
  551.3 12.2 fusion.157
  564.6 23.8 %fusion.158 = (f32[2,7,512]{2,1,0:T(8,128)S(1)}, f32[2,1,7,512,1024]{4,3,2,0,1:T(8,128)}) fusion(f32[2,512,7,1024]{3,1,2,0:T(8,128)} %fusion.157, f32[2,7,512]{2,1,0:T(8,128)S(1)} %dynamic-slice_bitcast_fusion.2, bf16[2,1024,1,64]{1,3,0,2:T(8,128)(2,1)S(1)} %get-tuple-element.461, bf16[2,1024,1,7,64]{1,4,3,0,2:T(8,128)(2,1)} %get-tuple-element.460, ...), kind=kOutput, calls=%fused_computation.26.clone.1 | convolution fusion | flops 976217088 | bytes 60481540 | tf_op jit(solution)/shard_map/while/body/eval_jaxpr/sicgd,sjcd->scgij/dot_general | solution.py:51
  588.4 24.6 %fusion.159 = bf16[2,7,512,1024]{3,2,1,0:T(8,128)(2,1)} fusion(f32[2,1,7,512,1024]{4,3,2,0,1:T(8,128)} %get-tuple-element.397, f32[2,512,7,1024]{3,1,2,0:T(8,128)} %fusion.157, f32[2,7,512]{2,1,0:T(8,128)S(1)} %get-tuple-element.398), kind=kLoop, calls=%fused_computation.29.clone.1 | loop fusion | flops 22020096 | bytes 73428992 | tf_op jit(solution)/shard_map/reshape.31
  613.0 8.3 fusion.160
  621.3 12.3 fusion.161
  633.7 10.8 fusion.162
  651.5 16.4 convolution_bitcast_fusion.2
  667.9 6.6 copy.211
  683.6 6.4 convolution_bitcast_fusion.5
  691.2 35.6 %all-to-all-done.4 = bf16[2,2,229376]{2,1,0:T(2,128)(2,1)S(1)} async-done(((bf16[2,2,229376]{2,1,0:T(2,128)(2,1)}), bf16[2,2,229376]{2,1,0:T(2,128)(2,1)S(1)}, u32[]{:S(2)}, u32[]{:S(2)}) %all-to-all-start.4) | async-done | bytes 1835040 | tf_op jit(solution)/shard_map/all_to_all | solution.py:215
  730.4 8.0 copy.179
  771.3 1044.1 %fusion.105 = (f32[32,1152]{1,0:T(8,128)S(1)}, f32[32,896]{1,0:T(8,128)}, f32[32,4864]{1,0:T(8,128)S(1)}, f32[32,4864]{1,0:T(8,128)S(1)}) fusion(f32[896,1152]{1,0:T(8,128)} %convolution_bitcast_fusion.4, f32[896,896]{1,0:T(8,128)} %convolution_bitcast_fusion.5, f32[896,4864]{1,0:T(8,128)} %convolution_bitcast_fusion.3, ...), kind=kCustom, calls=%all-reduce-scatter.4 | all-reduce-scatter fusion | flops 12058625 | bytes 43712512
  1816.4 12.5 collective-permute-start.6
  1838.8 17.3 add_convert_fusion.1
  1876.9 12.7 collective-permute-start.1
  1889.7 9.2 collective-permute-start
  1902.1 5.4 collective-permute-start.14
  1922.7 62.3 %all-reduce.15 = (f32[1152]{0:T(1024)S(1)}, f32[896]{0:T(1024)S(1)}, f32[896]{0:T(1024)S(1)}) all-reduce(f32[1152]{0:T(1024)S(1)} %convert_reduce_fusion, f32[896]{0:T(1024)S(1)} %get-tuple-element.210, f32[896]{0:T(1024)S(1)} %copy-done.46), channel_id=3, replica_groups=mesh['fsdp'=16,'seq'=2] {'fsdp','seq'}, use_global_device_ids=true, to_apply=%region_13.14.clone | all-reduce | flops 2944 | bytes 23552
  1997.2 20.2 concatenate.56
  2017.4 20.2 concatenate.57
  (272 shorter events, 233.0 us)
Async XLA Ops:
  7.2 48.8 %copy-start.13 = (bf16[2,512,896]{2,1,0:T(8,128)(2,1)S(1)}, bf16[2,512,896]{2,1,0:T(8,128)(2,1)}, u32[]{:S(2)}) copy-start(bf16[2,512,896]{2,1,0:T(8,128)(2,1)} %param.15) | copy-start | bytes 5505028
  7.2 48.8 %all-gather.6.cloned.1.call-start = ((), (), s32[]{:S(2)}) async-start(), calls=%async_computation.7 | async-start | bytes 2193408 | tf_op jit(solution)/shard_map/all_gather | solution.py:83
  7.9 251.6 %all-gather.8.cloned.1.call-start = ((), (), s32[]{:S(2)}) async-start(), calls=%async_computation.8 | async-start | bytes 1705984 | tf_op jit(solution)/shard_map/all_gather | solution.py:85
  8.7 259.1 %all-gather.14.cloned.1.call-start = ((), (), s32[]{:S(2)}) async-start(), calls=%async_computation.11 | async-start | bytes 9261056 | tf_op jit(solution)/shard_map/all_gather | solution.py:91
  9.4 275.4 %all-gather.12.cloned.1.call-start = ((), (), s32[]{:S(2)}) async-start(), calls=%async_computation.10 | async-start | bytes 9261056 | tf_op jit(solution)/shard_map/all_gather | solution.py:90
  53.2 22.9 %copy-start.19 = (f32[2,512,64]{1,2,0:T(8,128)}, f32[2,512,64]{1,2,0:T(8,128)S(1)}, u32[]{:S(2)}) copy-start(f32[2,512,64]{1,2,0:T(8,128)S(1)} %get-tuple-element.277) | copy-start | bytes 786436
  53.3 22.9 %copy-start.22 = (f32[2,512,64]{1,2,0:T(8,128)}, f32[2,512,64]{1,2,0:T(8,128)S(1)}, u32[]{:S(2)}) copy-start(f32[2,512,64]{1,2,0:T(8,128)S(1)} %get-tuple-element.278) | copy-start | bytes 786436
  69.9 10.6 all-to-all-start.1
  80.5 23.9 %all-to-all-start = ((bf16[2,512,14,64]{1,3,0,2:T(8,128)(2,1)}), bf16[2,512,14,64]{1,3,0,2:T(8,128)(2,1)S(1)}, u32[]{:S(2)}, u32[]{:S(2)}) async-start(bf16[2,512,14,64]{1,3,0,2:T(8,128)(2,1)} %copy.157), calls=%async_computation | async-start | bytes 3670016 | tf_op jit(solution)/shard_map/all_to_all | solution.py:110
  84.2 243.5 %all-gather.10.cloned.1.call-start = ((), (), s32[]{:S(2)}) async-start(), calls=%async_computation.9 | async-start | bytes 9261056 | tf_op jit(solution)/shard_map/all_gather | solution.py:89
  133.0 18.1 copy-start
  179.1 18.5 copy-start
  207.9 15.1 copy-start.50
  223.0 23.5 %all-to-all-start.2 = ((bf16[2,2,229376]{2,1,0:T(2,128)(2,1)}), bf16[2,2,229376]{2,1,0:T(2,128)(2,1)S(1)}, u32[]{:S(2)}, u32[]{:S(2)}) async-start(bf16[2,2,229376]{2,1,0:T(2,128)(2,1)} %reshape.324), calls=%async_computation.2 | async-start | bytes 3670016 | tf_op jit(solution)/shard_map/all_to_all | solution.py:132
  284.8 42.9 %copy-start.26 = (bf16[2,512,896]{2,1,0:T(8,128)(2,1)S(1)}, bf16[2,512,896]{2,1,0:T(8,128)(2,1)}, u32[]{:S(2)}) copy-start(bf16[2,512,896]{2,1,0:T(8,128)(2,1)} %multiply_convert_fusion.4) | copy-start | bytes 5505028
  359.6 17.0 copy-start.10
  406.0 37.5 %all-to-all-start.3 = ((bf16[2,512,14,64]{1,3,0,2:T(8,128)(2,1)}), bf16[2,512,14,64]{1,3,0,2:T(8,128)(2,1)S(1)}, u32[]{:S(2)}, u32[]{:S(2)}) async-start(bf16[2,512,14,64]{1,3,0,2:T(8,128)(2,1)} %copy.172), calls=%async_computation.3 | async-start | bytes 3670016 | tf_op jit(solution)/shard_map/all_to_all | solution.py:178
  409.7 1631.9 %reduce-scatter.13.cloned.1.call-start = ((), (), s32[]{:S(2)}) async-start(), calls=%async_computation.12 | async-start | bytes 17977344
  648.0 31.9 %all-to-all-start.5 = ((bf16[2,1024,1,128]{3,0,2,1:T(2,128)(2,1)}), bf16[2,1024,1,128]{3,0,2,1:T(2,128)(2,1)S(1)}, u32[]{:S(2)}, u32[]{:S(2)}) async-start(bf16[2,1024,1,128]{3,0,2,1:T(2,128)(2,1)} %pad_maximum_fusion.3), calls=%async_computation.5 | async-start | bytes 1048576 | tf_op jit(solution)/shard_map/all_to_all | solution.py:216
  651.5 16.4 copy-start.18
  679.9 47.0 %all-to-all-start.4 = ((bf16[2,2,229376]{2,1,0:T(2,128)(2,1)}), bf16[2,2,229376]{2,1,0:T(2,128)(2,1)S(1)}, u32[]{:S(2)}, u32[]{:S(2)}) async-start(bf16[2,2,229376]{2,1,0:T(2,128)(2,1)} %reshape.326), calls=%async_computation.4 | async-start | bytes 3670016 | tf_op jit(solution)/shard_map/all_to_all | solution.py:215
  691.2 74.2 %copy-start.27 = (bf16[2,512,128]{2,1,0:T(8,128)(2,1)}, bf16[2,512,128]{2,1,0:T(8,128)(2,1)S(1)}, u32[]{:S(2)}) copy-start(bf16[2,512,128]{2,1,0:T(8,128)(2,1)S(1)} %copy.189) | copy-start | bytes 786436
  1816.3 56.5 %copy-start.17 = (bf16[2,512,896]{2,1,0:T(8,128)(2,1)S(1)}, bf16[2,512,896]{2,1,0:T(8,128)(2,1)}, u32[]{:S(2)}) copy-start(bf16[2,512,896]{2,1,0:T(8,128)(2,1)} %copy-done.16) | copy-start | bytes 5505028
  1816.3 56.5 %copy-start.28 = (bf16[2,512,128]{2,1,0:T(8,128)(2,1)S(1)}, bf16[2,512,128]{2,1,0:T(8,128)(2,1)}, u32[]{:S(2)}) copy-start(bf16[2,512,128]{2,1,0:T(8,128)(2,1)} %copy-done.27) | copy-start | bytes 786436
  1816.4 56.5 %copy-start.48 = (bf16[896,1152]{1,0:T(8,128)(2,1)S(1)}, bf16[896,1152]{1,0:T(8,128)(2,1)}, u32[]{:S(2)}) copy-start(bf16[896,1152]{1,0:T(8,128)(2,1)} %all-gather.6.cloned.1.call-done) | copy-start | bytes 6193156
  1816.4 45.9 %collective-permute-start.6 = (f32[32,896]{1,0:T(8,128)}, f32[32,896]{1,0:T(8,128)S(1)}, u32[]{:S(2)}, u32[]{:S(2)}) collective-permute-start(f32[32,896]{1,0:T(8,128)} %get-tuple-element.257), channel_id=1, source_target_pairs={{0,3},{1,4},{2,5},{3,6},{4,7},{5,8},{6,9},{7,10},{8,11},{9,12},{10... | collective-permute-start | bytes 344072
  1828.9 37.1 %collective-permute-start.5 = (f32[32,896]{1,0:T(8,128)}, f32[32,896]{1,0:T(8,128)S(1)}, u32[]{:S(2)}, u32[]{:S(2)}) collective-permute-start(f32[32,896]{1,0:T(8,128)} %get-tuple-element.257), channel_id=1, source_target_pairs={{0,2},{1,3},{2,4},{3,5},{4,6},{5,7},{6,8},{7,9},{8,10},{9,11},{10,... | collective-permute-start | bytes 344072
  1831.6 37.8 %collective-permute-start.4 = (f32[32,896]{1,0:T(8,128)}, f32[32,896]{1,0:T(8,128)S(1)}, u32[]{:S(2)}, u32[]{:S(2)}) collective-permute-start(f32[32,896]{1,0:T(8,128)} %get-tuple-element.257), channel_id=1, source_target_pairs={{0,1},{1,2},{2,3},{3,4},{4,5},{5,6},{6,7},{7,8},{8,9},{9,10},{10,1... | collective-permute-start | bytes 344072
  1835.4 23.9 %collective-permute-start.7 = (f32[28,896]{1,0:T(8,128)S(1)}, f32[28,896]{1,0:T(8,128)S(1)}, u32[]{:S(2)}, u32[]{:S(2)}) collective-permute-start(f32[28,896]{1,0:T(8,128)S(1)} %slice.77), channel_id=1, source_target_pairs={{0,4},{1,5},{2,6},{3,7},{4,8},{5,9},{6,10},{7,11},{8,12},{9,13},{1... | collective-permute-start | bytes 301064
  1856.2 33.5 %collective-permute-start.2 = (f32[32,1152]{1,0:T(8,128)S(1)}, f32[32,1152]{1,0:T(8,128)S(1)}, u32[]{:S(2)}, u32[]{:S(2)}) collective-permute-start(f32[32,1152]{1,0:T(8,128)S(1)} %get-tuple-element.256), channel_id=1, source_target_pairs={{0,3},{1,4},{2,5},{3,6},{4,7},{5,8},{6,9},{7,10},{8,11},{9,12},{10... | collective-permute-start | bytes 442376
  1859.3 60.7 %copy-start.41 = (f32[2,512]{1,0:T(2,128)S(1)}, f32[2,512]{1,0:T(2,128)}, u32[]{:S(2)}) copy-start(f32[2,512]{1,0:T(2,128)} %get-tuple-element.279) | copy-start | bytes 12292
  1859.3 16.7 copy-start.40
  1859.3 53.4 %collective-permute-start.10 = (f32[32,4864]{1,0:T(8,128)S(1)}, f32[32,4864]{1,0:T(8,128)S(1)}, u32[]{:S(2)}, u32[]{:S(2)}) collective-permute-start(f32[32,4864]{1,0:T(8,128)S(1)} %get-tuple-element.258), channel_id=1, source_target_pairs={{0,3},{1,4},{2,5},{3,6},{4,7},{5,8},{6,9},{7,10},{8,11},{9,12},{10... | collective-permute-start | bytes 1867784
  1862.3 54.4 %collective-permute-start.9 = (f32[32,4864]{1,0:T(8,128)S(1)}, f32[32,4864]{1,0:T(8,128)S(1)}, u32[]{:S(2)}, u32[]{:S(2)}) collective-permute-start(f32[32,4864]{1,0:T(8,128)S(1)} %get-tuple-element.258), channel_id=1, source_target_pairs={{0,2},{1,3},{2,4},{3,5},{4,6},{5,7},{6,8},{7,9},{8,10},{9,11},{10,... | collective-permute-start | bytes 1867784
  1866.0 10.9 collective-permute-start.3
  1869.4 38.2 %collective-permute-start.11 = (f32[28,4864]{1,0:T(8,128)S(1)}, f32[28,4864]{1,0:T(8,128)S(1)}, u32[]{:S(2)}, u32[]{:S(2)}) collective-permute-start(f32[28,4864]{1,0:T(8,128)S(1)} %slice.78), channel_id=1, source_target_pairs={{0,4},{1,5},{2,6},{3,7},{4,8},{5,9},{6,10},{7,11},{8,12},{9,13},{1... | collective-permute-start | bytes 1634312
  1872.8 47.1 %copy-start.8 = (f32[2,512,896]{2,1,0:T(8,128)S(1)}, f32[2,512,896]{2,1,0:T(8,128)}, u32[]{:S(2)}) copy-start(f32[2,512,896]{2,1,0:T(8,128)} %copy-done.7) | copy-start | bytes 11010052
  1876.9 45.4 %copy-start.34 = (f32[28,1152]{1,0:T(8,128)}, f32[28,1152]{1,0:T(8,128)S(1)}, u32[]{:S(2)}) copy-start(f32[28,1152]{1,0:T(8,128)S(1)} %collective-permute-done.3) | copy-start | bytes 387076
  1876.9 22.0 %collective-permute-start.1 = (f32[32,1152]{1,0:T(8,128)S(1)}, f32[32,1152]{1,0:T(8,128)S(1)}, u32[]{:S(2)}, u32[]{:S(2)}) collective-permute-start(f32[32,1152]{1,0:T(8,128)S(1)} %get-tuple-element.256), channel_id=1, source_target_pairs={{0,2},{1,3},{2,4},{3,5},{4,6},{5,7},{6,8},{7,9},{8,10},{9,11},{10,... | collective-permute-start | bytes 442376
  1889.6 32.6 %copy-start.33 = (f32[32,1152]{1,0:T(8,128)}, f32[32,1152]{1,0:T(8,128)S(1)}, u32[]{:S(2)}) copy-start(f32[32,1152]{1,0:T(8,128)S(1)} %collective-permute-done.2) | copy-start | bytes 442372
  1889.7 12.5 collective-permute-start
  1898.9 23.4 %copy-start.35 = (f32[32,1152]{1,0:T(8,128)}, f32[32,1152]{1,0:T(8,128)S(1)}, u32[]{:S(2)}) copy-start(f32[32,1152]{1,0:T(8,128)S(1)} %collective-permute-done.1) | copy-start | bytes 442372
  1898.9 98.3 %collective-permute-start.8 = (f32[32,4864]{1,0:T(8,128)S(1)}, f32[32,4864]{1,0:T(8,128)}, u32[]{:S(2)}, u32[]{:S(2)}) collective-permute-start(f32[32,4864]{1,0:T(8,128)S(1)} %get-tuple-element.258), channel_id=1, source_target_pairs={{0,1},{1,2},{2,3},{3,4},{4,5},{5,6},{6,7},{7,8},{8,9},{9,10},{10,1... | collective-permute-start | bytes 1867784
  1902.1 20.1 copy-start.36
  1902.1 115.2 %collective-permute-start.14 = (f32[32,4864]{1,0:T(8,128)S(1)}, f32[32,4864]{1,0:T(8,128)}, u32[]{:S(2)}, u32[]{:S(2)}) collective-permute-start(f32[32,4864]{1,0:T(8,128)S(1)} %get-tuple-element.259), channel_id=1, source_target_pairs={{0,3},{1,4},{2,5},{3,6},{4,7},{5,8},{6,9},{7,10},{8,11},{9,12},{10... | collective-permute-start | bytes 1867784
  1907.6 109.8 %collective-permute-start.13 = (f32[32,4864]{1,0:T(8,128)S(1)}, f32[32,4864]{1,0:T(8,128)}, u32[]{:S(2)}, u32[]{:S(2)}) collective-permute-start(f32[32,4864]{1,0:T(8,128)S(1)} %get-tuple-element.259), channel_id=1, source_target_pairs={{0,2},{1,3},{2,4},{3,5},{4,6},{5,7},{6,8},{7,9},{8,10},{9,11},{10,... | collective-permute-start | bytes 1867784
  1912.7 104.7 %collective-permute-start.12 = (f32[32,4864]{1,0:T(8,128)S(1)}, f32[32,4864]{1,0:T(8,128)}, u32[]{:S(2)}, u32[]{:S(2)}) collective-permute-start(f32[32,4864]{1,0:T(8,128)S(1)} %get-tuple-element.259), channel_id=1, source_target_pairs={{0,1},{1,2},{2,3},{3,4},{4,5},{5,6},{6,7},{7,8},{8,9},{9,10},{10,1... | collective-permute-start | bytes 1867784
  1916.8 100.6 %collective-permute-start.15 = (f32[28,4864]{1,0:T(8,128)}, f32[28,4864]{1,0:T(8,128)}, u32[]{:S(2)}, u32[]{:S(2)}) collective-permute-start(f32[28,4864]{1,0:T(8,128)} %slice.79), channel_id=1, source_target_pairs={{0,4},{1,5},{2,6},{3,7},{4,8},{5,9},{6,10},{7,11},{8,12},{9,13},{1... | collective-permute-start | bytes 1634312
  (34 other events, 224.4 us)
Sparse Core Ops, SparseCore 0:
  10.2 44.1 all-gather.5
  56.5 38.5 all-gather.7
  97.3 75.8 all-gather.13
  175.2 75.2 all-gather.11
  252.5 75.1 all-gather.9
  427.3 472.5 reduce-scatter.12
where the time goes:
time: 2060 us; the launch traced here: 2050 us
  blocking collectives  1140 us (55%)
  matrix products  380 us (18%)
  local copies, waits for them, and re-layouts  192 us (9%)
  other arithmetic  111 us (5%)
  starting transfers between devices  103 us (5%)
  waiting for transfers between devices  94.5 us (5%)
    unnamed x3, blocking collectives  1140 us
    unnamed x128, local copies, waits for them, and re-layouts  87.8 us
    unnamed x17, starting transfers between devices  81.4 us
    dot_general x4, matrix products, masked_scores(): jnp.einsum('sicgd,sjcd->scgij', rows, key_full, preferred_element_type=jn...  76.6 us
    another operation x7, other arithmetic  54.5 us
  transfers between devices with their start and end apart: 28, of which 6 were waited for; matrix products, arithmetic and copies ran while one was open for 80% of the time, Pallas kernels for 0%

commit v1 on v0

v1 whole, which is shorter than its diff:
```python
import functools

import jax
import jax.numpy as jnp
from jax import lax
from jax.experimental import pallas as pl
from jax.experimental.pallas import tpu as pltpu
from jax.sharding import PartitionSpec as P

HEADS = 14
KV_HEADS = 2
HEAD_DIM = 64
GROUP = HEADS // KV_HEADS
PAIRS = HEADS // 2
LANES = 128
BLOCK = 256
CHUNK = 256
EPS = 1e-06
THETA = 1000000.0
BF16 = jnp.bfloat16
F32 = jnp.float32
VMEM_LIMIT = 60 * 1024 * 1024

NN = (((1,), (0,)), ((), ()))
NT = (((1,), (1,)), ((), ()))
TN = (((0,), (0,)), ((), ()))


def mm(left, right, dims=NN):
    return lax.dot_general(left, right, dims, preferred_element_type=F32)


def params():
    return pltpu.CompilerParams(vmem_limit_bytes=VMEM_LIMIT)


def swap_halves(values):
    lane = lax.broadcasted_iota(jnp.int32, values.shape, 1)
    half = HEAD_DIM // 2
    ahead = pltpu.roll(values, LANES - half, 1)
    behind = pltpu.roll(values, half, 1)
    return jnp.where(lane % HEAD_DIM < half, ahead, behind)


def qkv_kernel(x_ref, gain_ref, weight_ref, bias_ref, cos_ref, sin_ref, normed_ref, query_ref, pair_ref):
    x = x_ref[...].astype(F32)
    scale = lax.rsqrt(jnp.mean(x * x, axis=-1, keepdims=True) + EPS)
    normed = (x * scale * gain_ref[...].astype(F32)).astype(BF16)
    normed_ref[...] = normed
    pre = mm(normed, weight_ref[...]) + bias_ref[...].astype(F32)
    cosine, sine = cos_ref[...], sin_ref[...]
    qwidth = HEADS * HEAD_DIM
    for tile in range(PAIRS):
        part = pre[:, tile * LANES : (tile + 1) * LANES]
        turned = part * cosine + swap_halves(part) * sine
        query_ref[:, tile * LANES : (tile + 1) * LANES] = turned.astype(BF16)
    part = pre[:, qwidth : qwidth + LANES]
    pair_ref[:, :LANES] = (part * cosine + swap_halves(part) * sine).astype(BF16)
    pair_ref[:, LANES:] = pre[:, qwidth + LANES :].astype(BF16)


def split_heads(block):
    wide = block.astype(F32)
    lane = lax.broadcasted_iota(jnp.int32, wide.shape, 1)
    first = jnp.where(lane < HEAD_DIM, wide, 0.0)
    second = jnp.where(lane < HEAD_DIM, pltpu.roll(wide, HEAD_DIM, 1), 0.0)
    return first, second


def join_heads(first, second):
    lane = lax.broadcasted_iota(jnp.int32, first.shape, 1)
    return jnp.where(lane < HEAD_DIM, first, pltpu.roll(second, HEAD_DIM, 1))


def attend_kernel(length, query_ref, key_ref, value_ref, mixed_ref, log_ref):
    pair = pl.program_id(1)
    scale = HEAD_DIM**-0.5
    heads = [part.astype(BF16) for part in split_heads(query_ref[0])]
    lane = lax.broadcasted_iota(jnp.int32, (BLOCK, LANES), 1)
    row = lax.broadcasted_iota(jnp.int32, (BLOCK, BLOCK), 0)
    col = lax.broadcasted_iota(jnp.int32, (BLOCK, BLOCK), 1)
    for index in range(length // BLOCK):
        rows = slice(index * BLOCK, (index + 1) * BLOCK)
        seen = index * BLOCK
        outs = []
        for which in range(2):
            head = 2 * pair + which
            kv = head // GROUP
            query = heads[which][rows]
            keys = key_ref[0, kv]
            diagonal = mm(query, keys[rows], NT) * scale
            diagonal = jnp.where(row >= col, diagonal, -1e30)
            top = jnp.max(diagonal, axis=-1, keepdims=True)
            if seen:
                before = mm(query, keys[:seen], NT) * scale
                top = jnp.maximum(top, jnp.max(before, axis=-1, keepdims=True))
            probs = jnp.exp(diagonal - top).astype(BF16)
            mixed = mm(probs, value_ref[0, kv, rows, :])
            if seen:
                probs = jnp.exp(before - top).astype(BF16)
                mixed = mixed + mm(probs, value_ref[0, kv, :seen, :])
            total = mixed[:, HEAD_DIM : HEAD_DIM + 1]
            outs.append(mixed / total)
            kept = jnp.where(lane == head, top + jnp.log(total), log_ref[0, rows, :])
            log_ref[0, rows, :] = kept
        mixed_ref[0, rows, :] = join_heads(outs[0], outs[1]).astype(BF16)


def widen(values, column):
    lane = lax.broadcasted_iota(jnp.int32, values.shape, 1)
    high = column.astype(BF16).astype(F32)
    middle = (column - high).astype(BF16).astype(F32)
    low = column - high - middle
    values = jnp.where(lane == HEAD_DIM, high, values)
    values = jnp.where(lane == HEAD_DIM + 1, middle, values)
    return jnp.where(lane == HEAD_DIM + 2, low, values).astype(BF16)


def back_kernel(length, query_ref, grad_ref, mixed_ref, log_ref, key_ref, value_ref, d_query_ref, d_key_ref, d_value_ref):
    pair = pl.program_id(1)
    scale = HEAD_DIM**-0.5

    @pl.when(pair == 0)
    def start():
        d_key_ref[...] = jnp.zeros_like(d_key_ref)
        d_value_ref[...] = jnp.zeros_like(d_value_ref)

    queries = split_heads(query_ref[0])
    grads = split_heads(grad_ref[0])
    mixes = split_heads(mixed_ref[0])
    lane = lax.broadcasted_iota(jnp.int32, (length, LANES), 1)
    row = lax.broadcasted_iota(jnp.int32, (BLOCK, BLOCK), 0)
    col = lax.broadcasted_iota(jnp.int32, (BLOCK, BLOCK), 1)
    outs = []
    for which in range(2):
        head = 2 * pair + which
        kv = head // GROUP
        log_total = jnp.sum(jnp.where(lane == head, log_ref[0], 0.0), axis=-1, keepdims=True)
        inner = jnp.sum(grads[which] * mixes[which], axis=-1, keepdims=True)
        query = widen(queries[which] * scale, -log_total)
        query_low = queries[which].astype(BF16)
        grad = widen(grads[which], -inner)
        grad_low = grads[which].astype(BF16)
        parts = [None] * (length // BLOCK)
        for index in range(length // BLOCK):
            own = slice(index * BLOCK, (index + 1) * BLOCK)
            keys, values = key_ref[0, kv, own, :], value_ref[0, kv, own, :]
            key_sum = value_sum = None
            for other in range(index, length // BLOCK):
                rows = slice(other * BLOCK, (other + 1) * BLOCK)
                scores = mm(keys, query[rows], NT)
                if other == index:
                    scores = jnp.where(row <= col, scores, -1e30)
                probs = jnp.exp(scores)
                d_scores = (probs * mm(values, grad[rows], NT)).astype(BF16)
                value_part = mm(probs.astype(BF16), grad_low[rows])
                key_part = mm(d_scores, query_low[rows])
                key_sum = key_part if key_sum is None else key_sum + key_part
                value_sum = value_part if value_sum is None else value_sum + value_part
                part = mm(d_scores, keys, TN)
                parts[other] = part if parts[other] is None else parts[other] + part
            d_key_ref[0, kv, own, :] += key_sum * scale
            d_value_ref[0, kv, own, :] += value_sum
        outs.append(parts)
    for index in range(length // BLOCK):
        rows = slice(index * BLOCK, (index + 1) * BLOCK)
        joined = join_heads(outs[0][index], outs[1][index]) * scale
        d_query_ref[0, rows, :] = joined.astype(BF16)


def plain_feed_kernel(
    normed_ref, turned_ref, cot_ref, gate_ref, up_ref, down_ref,
    result_ref, d_normed_ref, gate_grad_ref, up_grad_ref, down_grad_ref,
):
    @pl.when(pl.program_id(0) == 0)
    def start():
        result_ref[...] = jnp.zeros_like(result_ref)
        d_normed_ref[...] = jnp.zeros_like(d_normed_ref)

    normed, cot = normed_ref[...], cot_ref[...]
    gate_weight, up_weight, down_weight = gate_ref[...], up_ref[...], down_ref[...]
    gate = mm(normed, gate_weight)
    up = mm(normed, up_weight)
    d_act = mm(cot, down_weight, NT)
    sigma = jax.nn.sigmoid(gate)
    silu = gate * sigma
    act = (silu * up).astype(BF16)
    d_gate = (d_act * up * sigma * (1.0 + gate * (1.0 - sigma))).astype(BF16)
    d_up = (d_act * silu).astype(BF16)
    result_ref[...] += mm(act, down_weight)
    d_normed_ref[...] += mm(d_gate, gate_weight, NT) + mm(d_up, up_weight, NT)
    turned = turned_ref[...]
    gate_grad_ref[...] = mm(turned, d_gate).astype(gate_grad_ref.dtype)
    up_grad_ref[...] = mm(turned, d_up).astype(up_grad_ref.dtype)
    down_grad_ref[...] = mm(act, cot, TN).astype(down_grad_ref.dtype)


MESH = pl.DeviceIdType.MESH
ANY = pl.BlockSpec(memory_space=pl.ANY)


class Ring:
    def __init__(self, chips):
        self.n = chips
        self.core = lax.rem(lax.axis_index("fsdp"), 2)
        self.chip = lax.div(lax.axis_index("fsdp"), 2)
        self.mine = lax.axis_index("seq")
        side, line = lax.rem(self.chip, 2), lax.div(self.chip, 2)
        self.rank = line * (1 - side) + (chips - 1 - line) * side
        self.right = {"fsdp": 2 * self.chip_at(1) + self.core}
        self.left = {"fsdp": 2 * self.chip_at(-1) + self.core}
        self.partner = {"fsdp": 2 * self.chip + 1 - self.core}
        self.peer = {"seq": 1 - self.mine}

    def chip_at(self, offset):
        rank = lax.rem(self.rank + 2 * self.n + offset, self.n)
        side = lax.div(rank, self.n // 2)
        line = rank * (1 - side) + (self.n - 1 - rank) * side
        return 2 * line + side

    def greet(self, others):
        barrier = pltpu.get_barrier_semaphore()
        for other in others:
            pl.semaphore_signal(barrier, inc=1, device_id=other, device_id_type=MESH)
        pl.semaphore_wait(barrier, len(others))


def remote(src, dst, send, recv, device):
    return pltpu.make_async_remote_copy(
        src_ref=src, dst_ref=dst, send_sem=send, recv_sem=recv, device_id=device, device_id_type=MESH
    )


class Gather:
    def __init__(self, ring, pieces, sems):
        self.ring, self.pieces, self.sems = ring, pieces, sems

    def refs(self, piece, hop):
        direction, own, block = self.pieces[piece][:3]
        dst = block(self.ring.chip_at(-direction * hop))
        return (own if hop == 0 else dst), dst

    def along(self, piece, hop):
        src, dst = self.refs(piece, hop)
        target = self.ring.right if self.pieces[piece][0] > 0 else self.ring.left
        return remote(src, dst, self.sems[0].at[piece, hop], self.sems[1].at[piece, hop], target)

    def mirror(self, piece, hop):
        src, dst = self.refs(piece, hop)
        return remote(src, dst, self.sems[2].at[piece, hop], self.sems[3].at[piece, hop], self.pieces[piece][3])

    def mirrored(self, piece, hop):
        return self.pieces[piece][3] is not None and self.pieces[piece][4] <= hop <= self.pieces[piece][5]

    def advance(self, hop, pieces):
        for piece in pieces:
            reach = self.pieces[piece][5]
            if 0 < hop <= reach:
                self.along(piece, hop - 1).wait_recv()
            if hop < reach:
                self.along(piece, hop).start()
            if self.mirrored(piece, hop):
                self.mirror(piece, hop).start()

    def finish(self):
        for piece in range(len(self.pieces)):
            for hop in range(self.ring.n):
                if hop < self.pieces[piece][5]:
                    self.along(piece, hop).wait_send()
                if self.mirrored(piece, hop):
                    self.mirror(piece, hop).wait()


def gather_sems(pieces):
    return [pltpu.SemaphoreType.DMA((pieces, CHIPS)) for _ in range(4)]


class Reduce:
    def __init__(self, ring, pieces, buffers, sems):
        self.ring, self.pieces, self.buffers, self.sems = ring, pieces, buffers, sems

    def chip(self, piece, hop):
        return self.ring.chip_at(self.pieces[piece][0] * (self.pieces[piece][5] - hop))

    def give(self, piece, hop):
        src = self.pieces[piece][2](self.chip(piece, hop))
        dst = self.buffers[piece][2].at[hop]
        return remote(src, dst, self.sems[2].at[piece, hop], self.sems[3].at[piece, hop], self.pieces[piece][3])

    def along(self, piece, hop):
        send, recv = self.buffers[piece][:2]
        src = self.pieces[piece][1](self.chip(piece, 0)) if hop == 0 and self.alone(piece) else send.at[hop % 2]
        target = self.ring.right if self.pieces[piece][0] > 0 else self.ring.left
        return remote(src, recv.at[hop], self.sems[0].at[piece, hop], self.sems[1].at[piece, hop], target)

    def alone(self, piece):
        return self.pieces[piece][2] is None

    def begin(self):
        self.offer(0, range(len(self.pieces)))

    def given(self, piece, hop):
        reach, kept = self.pieces[piece][5:]
        return not self.alone(piece) and (hop < reach or hop == reach and kept)

    def offer(self, hop, pieces):
        for piece in pieces:
            if self.given(piece, hop):
                self.give(piece, hop).start()

    def advance(self, hop, pieces):
        for piece in pieces:
            reach, kept = self.pieces[piece][5:]
            send, recv, land = self.buffers[piece]
            if not kept and hop == reach + 1:
                self.along(piece, reach - 1).wait_recv()
                self.pieces[piece][4][...] += recv[reach - 1].astype(F32)
            if hop > reach or hop == reach and not kept:
                continue
            self.offer(hop + 1, [piece])
            if hop == 0 and self.alone(piece):
                self.along(piece, 0).start()
                continue
            if 2 <= hop < reach:
                self.along(piece, hop - 2).wait_send()
            addends = [self.pieces[piece][1](self.chip(piece, hop))[...].astype(F32)]
            if self.given(piece, hop):
                self.give(piece, hop).wait_recv()
                addends.append(land[hop].astype(F32))
            if hop > 0:
                self.along(piece, hop - 1).wait_recv()
                addends.append(recv[hop - 1].astype(F32))
            total = functools.reduce(lax.add, addends)
            if hop < reach:
                send[hop % 2] = total.astype(send.dtype)
                self.along(piece, hop).start()
            else:
                self.pieces[piece][4][...] = total

    def finish(self):
        for piece in range(len(self.pieces)):
            reach = self.pieces[piece][5]
            for hop in (reach - 2, reach - 1):
                self.along(piece, hop).wait_send()
            for hop in range(self.ring.n):
                if self.given(piece, hop):
                    self.give(piece, hop).wait_send()


def reduce_scratch(shapes):
    buffers = []
    for rows, columns, shared in shapes:
        buffers += [pltpu.VMEM((2, rows, columns), BF16), pltpu.VMEM((CHIPS - 1, rows, columns), BF16)]
        if shared:
            buffers.append(pltpu.VMEM((CHIPS, rows, columns), BF16))
    return buffers + [pltpu.SemaphoreType.DMA((len(shapes), CHIPS)) for _ in range(4)]


def make_reduce(ring, pieces, scratch):
    scratch = list(scratch)
    buffers = []
    for piece in pieces:
        send, recv = scratch.pop(0), scratch.pop(0)
        buffers.append((send, recv, None if piece[2] is None else scratch.pop(0)))
    return Reduce(ring, pieces, buffers, scratch)


class Share:
    def __init__(self, ring, part, out, scratch):
        self.ring, self.part, self.out = ring, part, out
        self.peer_send, self.peer_recv, self.core_send, self.core_recv, self.sems = scratch
        self.split = len(out.shape) == 4
        self.rows = out.shape[-2]

    def over_seq(self):
        return remote(self.peer_send, self.peer_recv, self.sems.at[0], self.sems.at[1], self.ring.peer)

    def over_core(self):
        return remote(self.core_send, self.core_recv, self.sems.at[2], self.sems.at[3], self.ring.partner)

    def owned(self, core, seq):
        start = (2 * core + seq) * self.rows
        return self.part[start : start + self.rows, :]

    def first(self):
        for mine in range(2):

            @pl.when(self.ring.mine == mine)
            def pick(mine=mine):
                for core in range(2):
                    self.peer_send[core] = self.owned(core, 1 - mine).astype(BF16)

        self.over_seq().start()

    def second(self):
        self.over_seq().wait()
        for mine in range(2):
            for core in range(2):

                @pl.when((self.ring.mine == mine) & (self.ring.core == core))
                def pick(mine=mine, core=core):
                    if self.split:
                        self.out[mine, core] = self.owned(core, mine)
                        self.out[1 - mine, core] = self.peer_recv[core].astype(F32)
                        self.core_send[mine] = self.owned(1 - core, mine).astype(BF16)
                        self.core_send[1 - mine] = self.peer_recv[1 - core]
                    else:
                        self.out[core] = self.owned(core, mine) + self.peer_recv[core].astype(F32)
                        give = self.owned(1 - core, mine) + self.peer_recv[1 - core].astype(F32)
                        self.core_send[0] = give.astype(BF16)

        self.over_core().start()

    def third(self):
        self.over_core().wait()
        if self.split:
            for seq in range(2):
                self.out[seq, 1 - self.ring.core] = self.core_recv[seq].astype(F32)
        else:
            self.out[1 - self.ring.core] = self.core_recv[0].astype(F32)


def share_scratch(rows, columns, split):
    both, last = (2, rows, columns), (2 if split else 1, rows, columns)
    return [
        pltpu.VMEM(both, BF16), pltpu.VMEM(both, BF16), pltpu.VMEM(last, BF16), pltpu.VMEM(last, BF16),
        pltpu.SemaphoreType.DMA((4,)),
    ]


class ShareRows:
    def __init__(self, ring, part, out, scratch):
        self.ring, self.part, self.out = ring, part, out
        self.send, self.recv, self.sems = scratch
        self.rows = out.shape[0]

    def over_seq(self):
        return remote(self.send, self.recv, self.sems.at[0], self.sems.at[1], self.ring.peer)

    def first(self):
        for mine in range(2):

            @pl.when(self.ring.mine == mine)
            def pick(mine=mine):
                start = (1 - mine) * self.rows
                self.send[...] = self.part[start : start + self.rows, :].astype(BF16)

        self.over_seq().start()

    def second(self):
        self.over_seq().wait()
        for mine in range(2):

            @pl.when(self.ring.mine == mine)
            def pick(mine=mine):
                start = mine * self.rows
                self.out[...] = self.part[start : start + self.rows, :] + self.recv[...].astype(F32)


def share_rows_scratch(rows, columns):
    one = (rows, columns)
    return [pltpu.VMEM(one, BF16), pltpu.VMEM(one, BF16), pltpu.SemaphoreType.DMA((2,))]


def spread(points, halves, now):
    plan = [[] for _ in range(points + 1)]
    steps = [(hop, half) for hop in range(CHIPS) for half in halves]
    plan[0] = steps[:now]
    rest = steps[now:]
    for index, step in enumerate(rest):
        plan[-(-(index + 1) * points // len(rest))].append(step)
    return plan


def at_point(step, first, plan, points, which, transfer):
    for place, moves in enumerate(plan[:-1]):
        if moves and place % points == which:

            @pl.when(step == first + place // points)
            def move(moves=moves):
                for hop, pieces in moves:
                    transfer.advance(hop, pieces)


def at_end(plan, transfer):
    for hop, pieces in plan[-1]:
        transfer.advance(hop, pieces)
    transfer.finish()


def rope_tables(positions):
    half = HEAD_DIM // 2
    freqs = THETA ** (-jnp.arange(0, HEAD_DIM, 2).astype(F32) / HEAD_DIM)
    angles = positions.astype(F32)[..., None] * freqs
    cosine, sine = jnp.cos(angles), jnp.sin(angles)
    return jnp.tile(cosine, (1, LANES // half)), jnp.tile(
        jnp.concatenate([-sine, sine], axis=-1), (1, LANES // HEAD_DIM)
    )


def rms_back(values, scale, gain, upstream):
    weighted = upstream * gain
    inner = jnp.mean(weighted * values, axis=-1, keepdims=True)
    grad_in = scale * weighted - values * (scale * scale * scale) * inner
    grad_gain = jnp.sum(upstream * values * scale, axis=0)
    return (grad_in, grad_gain)


def rotate_back(grads, cosine, sine):
    tokens, width = grads.shape
    tiles = grads.reshape(tokens, width // LANES, LANES)
    half = HEAD_DIM // 2
    lane = lax.iota(jnp.int32, LANES)
    ahead = jnp.concatenate([tiles[..., half:], tiles[..., :half]], axis=-1)
    behind = jnp.concatenate([tiles[..., -half:], tiles[..., :-half]], axis=-1)
    other = jnp.where(lane % HEAD_DIM < half, ahead, behind)
    return (tiles * cosine[:, None, :] - other * sine[:, None, :]).reshape(tokens, width)


def full(shape):
    return pl.BlockSpec(shape, lambda *_: (0,) * len(shape))


def plain_shards(
    inputs, positions, qkv_weight, qkv_bias, output_weight, first_gain,
    gate_weight, up_weight, down_weight, second_gain, cotangent,
):
    seqs, half_len, width = inputs.shape
    nseq = lax.axis_size("seq")
    length = half_len * nseq
    whole = seqs // nseq
    tokens = whole * length
    qwidth = HEADS * HEAD_DIM
    kvwidth = KV_HEADS * HEAD_DIM

    def gather(part):
        return lax.all_gather(part, "fsdp", axis=0, tiled=True)

    def to_sequences(part):
        return lax.all_to_all(part, "seq", split_axis=0, concat_axis=1, tiled=True)

    def to_tokens(part):
        return lax.all_to_all(part, "seq", split_axis=1, concat_axis=0, tiled=True)

    def scatter(grad):
        part = lax.psum_scatter(grad.astype(BF16), "fsdp", scatter_dimension=0, tiled=True)
        return lax.psum_scatter(part.astype(F32), "seq", scatter_dimension=0, tiled=True)

    x_low = to_sequences(inputs).reshape(tokens, width)
    places = to_sequences(positions).reshape(tokens)
    cot = to_sequences(cotangent).reshape(tokens, width)
    full_qkv, full_bias, full_output = gather(qkv_weight), gather(qkv_bias), gather(output_weight)
    gain1, gain2 = gather(first_gain), gather(second_gain)
    full_gate, full_up, full_down = gather(gate_weight), gather(up_weight), gather(down_weight)

    cosine, sine = rope_tables(places)
    normed1, query, pair = pl.pallas_call(
        qkv_kernel,
        grid=(tokens // BLOCK,),
        in_specs=[
            pl.BlockSpec((BLOCK, width), lambda i: (i, 0)),
            full((1, width)),
            full((width, qwidth + 2 * kvwidth)),
            full((1, qwidth + 2 * kvwidth)),
            pl.BlockSpec((BLOCK, LANES), lambda i: (i, 0)),
            pl.BlockSpec((BLOCK, LANES), lambda i: (i, 0)),
        ],
        out_specs=[
            pl.BlockSpec((BLOCK, width), lambda i: (i, 0)),
            pl.BlockSpec((BLOCK, qwidth), lambda i: (i, 0)),
            pl.BlockSpec((BLOCK, 2 * kvwidth), lambda i: (i, 0)),
        ],
        out_shape=[
            jax.ShapeDtypeStruct((tokens, width), BF16),
            jax.ShapeDtypeStruct((tokens, qwidth), BF16),
            jax.ShapeDtypeStruct((tokens, 2 * kvwidth), BF16),
        ],
        compiler_params=params(),
    )(x_low, gain1[None], full_qkv, full_bias[None], cosine, sine)

    query = query.reshape(whole, length, qwidth)
    pair = pair.reshape(whole, length, 2, KV_HEADS, HEAD_DIM).transpose(2, 0, 3, 1, 4)
    ones = jnp.ones((2, whole, KV_HEADS, length, 3), BF16)
    pair = jnp.pad(jnp.concatenate([pair, ones], axis=-1), ((0, 0),) * 4 + ((0, HEAD_DIM - 3),))
    keys, values = pair[0], pair[1]
    lanes_spec = pl.BlockSpec((1, length, LANES), lambda b, p: (b, 0, p))
    kv_spec = pl.BlockSpec((1, KV_HEADS, length, LANES), lambda b, p: (b, 0, 0, 0))
    log_spec = pl.BlockSpec((1, length, LANES), lambda b, p: (b, 0, 0))
    mixed, logs = pl.pallas_call(
        functools.partial(attend_kernel, length),
        grid=(whole, PAIRS),
        in_specs=[lanes_spec, kv_spec, kv_spec],
        out_specs=[lanes_spec, log_spec],
        out_shape=[
            jax.ShapeDtypeStruct((whole, length, qwidth), BF16),
            jax.ShapeDtypeStruct((whole, length, LANES), F32),
        ],
        compiler_params=params(),
    )(query, keys, values)

    mixed_tokens = mixed.reshape(tokens, qwidth)
    x = x_low.astype(F32)
    hidden = x + mm(mixed_tokens, full_output)
    gain2 = gain2.astype(F32)
    scale2 = lax.rsqrt(jnp.mean(hidden * hidden, axis=-1, keepdims=True) + EPS)
    normed2 = (hidden * scale2 * gain2).astype(BF16)

    ff = gate_weight.shape[1]
    column = pl.BlockSpec((width, CHUNK), lambda j: (0, j))
    line = pl.BlockSpec((CHUNK, width), lambda j: (j, 0))
    total, d_normed2, gate_grad, up_grad, down_grad = pl.pallas_call(
        plain_feed_kernel,
        grid=(ff // CHUNK,),
        in_specs=[full((tokens, width)), full((width, tokens)), full((tokens, width)), column, column, line],
        out_specs=[full((tokens, width)), full((tokens, width)), column, column, line],
        out_shape=[
            jax.ShapeDtypeStruct((tokens, width), F32),
            jax.ShapeDtypeStruct((tokens, width), F32),
            jax.ShapeDtypeStruct((width, ff), BF16),
            jax.ShapeDtypeStruct((width, ff), BF16),
            jax.ShapeDtypeStruct((ff, width), BF16),
        ],
        compiler_params=params(),
    )(normed2, normed2.T, cot, full_gate, full_up, full_down)

    result = to_tokens((hidden + total).astype(BF16).reshape(whole, length, width))
    back2, second_grad = rms_back(hidden, scale2, gain2, d_normed2)
    d_hidden = cot.astype(F32) + back2
    d_branch = d_hidden.astype(BF16)
    output_grad = mm(mixed_tokens, d_branch, TN)
    d_mixed = mm(d_branch, full_output, NT).astype(BF16).reshape(whole, length, qwidth)

    d_query, d_keys, d_values = pl.pallas_call(
        functools.partial(back_kernel, length),
        grid=(whole, PAIRS),
        in_specs=[lanes_spec, lanes_spec, lanes_spec, log_spec, kv_spec, kv_spec],
        out_specs=[lanes_spec, kv_spec, kv_spec],
        out_shape=[
            jax.ShapeDtypeStruct((whole, length, qwidth), BF16),
            jax.ShapeDtypeStruct((whole, KV_HEADS, length, LANES), F32),
            jax.ShapeDtypeStruct((whole, KV_HEADS, length, LANES), F32),
        ],
        compiler_params=params(),
    )(query, d_mixed, mixed, logs, keys, values)

    def merge(part):
        part = part[..., :HEAD_DIM].astype(BF16)
        return part.transpose(0, 2, 1, 3).reshape(tokens, kvwidth)

    turned = jnp.concatenate([d_query.reshape(tokens, qwidth), merge(d_keys)], axis=-1).astype(F32)
    turned = rotate_back(turned, cosine, sine).astype(BF16)
    d_pre = jnp.concatenate([turned, merge(d_values)], axis=-1)
    qkv_grad = mm(normed1, d_pre, TN)
    bias_grad = jnp.sum(d_pre.astype(F32), axis=0)
    d_normed1 = mm(d_pre, full_qkv, NT)
    scale1 = lax.rsqrt(jnp.mean(x * x, axis=-1, keepdims=True) + EPS)
    back1, first_grad = rms_back(x, scale1, gain1.astype(F32), d_normed1)
    input_grad = (d_hidden + back1).astype(BF16).reshape(whole, length, width)
    input_grad = to_tokens(input_grad).astype(F32)

    def scatter_small(grad):
        return lax.psum_scatter(grad, ("fsdp", "seq"), scatter_dimension=0, tiled=True)

    return (
        result,
        input_grad,
        scatter(qkv_grad),
        scatter_small(bias_grad),
        scatter(output_grad),
        scatter_small(first_grad),
        scatter(gate_grad),
        scatter(up_grad),
        scatter(down_grad),
        scatter_small(second_grad),
    )


CHIPS = 8
OWNERS = 4
SPLITS = (64, 88)
STARTS = (0, 64)
BITS = 16
QUARTER = 512
BOTH = 1024


def inside(shape):
    return pl.BlockSpec(shape, lambda *_: (0,) * len(shape), pipeline_mode=pl.Buffered(1))


def dma(*shape):
    return pltpu.SemaphoreType.DMA(shape)


def spans():
    return [2 * CHIPS * split for split in SPLITS]


def stack_rows(first, second):
    return jnp.concatenate([first.astype(F32), second.astype(F32)], axis=0)


def one_hot(rows, segments):
    row = lax.broadcasted_iota(jnp.int32, (rows, LANES), 0)
    col = lax.broadcasted_iota(jnp.int32, (rows, LANES), 1)
    found = None
    for a, b, shift in segments:
        here = (row - col == shift) & (col >= a) & (col < b)
        found = here if found is None else found | here
    return jnp.where(found, 1.0, 0.0).astype(BF16)


def owner_columns(core, group, section):
    own = sum(SPLITS)
    return (section // 2) * OWNERS * own + 2 * own * core + (section % 2) * own + STARTS[group]


def gather_columns(source, core, group, store):
    split = SPLITS[group]
    for tile in range(2 * CHIPS * split // LANES):
        segments, low, high = [], None, None
        for section in range(tile * LANES // split, ((tile + 1) * LANES - 1) // split + 1):
            a = max(section * split - tile * LANES, 0)
            b = min((section + 1) * split - tile * LANES, LANES)
            shift = owner_columns(core, group, section) + tile * LANES - section * split
            segments.append((a, b, shift))
            low = a + shift if low is None else low
            high = b + shift
        start = low // LANES * LANES
        count = -(-(high - start) // LANES) * LANES
        pick = one_hot(count, [(a, b, shift - start) for a, b, shift in segments])
        store(tile, mm(source[:, start : start + count], pick))


def spread_columns(sources, store, width):
    own = sum(SPLITS)
    for tile in range(width // LANES):
        total = None
        column = tile * LANES
        while column < (tile + 1) * LANES:
            chip, rest = divmod(column, OWNERS * own)
            core, rest = divmod(rest, 2 * own)
            seq, rest = divmod(rest, own)
            group = 0 if rest < SPLITS[0] else 1
            left = SPLITS[0] - rest if group == 0 else own - rest
            stop = min(column + left, (tile + 1) * LANES)
            index = (2 * chip + seq) * SPLITS[group] + rest - STARTS[group]
            start = index // LANES * LANES
            a, b = column - tile * LANES, stop - tile * LANES
            high = index + b - a
            count = -(-(high - start) // LANES) * LANES
            pick = one_hot(count, [(a, b, index - a - start)])
            part = mm(sources[group][core][:, start : start + count], pick)
            total = part if total is None else total + part
            column = stop
        store(tile, total)


def project(length, x_ref, table_ref, vectors_ref, weight_ref, turned_ref, query_ref, key_ref, value_ref):
    width = x_ref.shape[2]
    qwidth = HEADS * HEAD_DIM
    lane = lax.broadcasted_iota(jnp.int32, (BLOCK, LANES), 1)
    extra = (lane >= HEAD_DIM) & (lane < HEAD_DIM + 3)
    bias, gain = vectors_ref[0:1, :], vectors_ref[1:2, :width]
    early = weight_ref[0].reshape(width, BOTH)
    late = weight_ref[1, :, :, : qwidth + 2 * LANES - BOTH].reshape(width, qwidth + 2 * LANES - BOTH)
    for index in range(length // BLOCK):
        rows = slice(index * BLOCK, (index + 1) * BLOCK)
        half, start = index * BLOCK // (length // 2), index * BLOCK % (length // 2)
        x = x_ref[half, start : start + BLOCK, :].astype(F32)
        scale = lax.rsqrt(jnp.mean(x * x, axis=-1, keepdims=True) + EPS)
        normed = (x * scale * gain).astype(BF16)
        turned_ref[:, rows] = normed.T
        pre = mm(normed, early) + bias[:, :BOTH]
        values = mm(normed, late) + bias[:, BOTH:]
        cosine, sine = tables(table_ref[half, start : start + BLOCK, :])
        for tile in range(PAIRS):
            columns = slice(tile * LANES, (tile + 1) * LANES)
            part = pre[:, columns]
            query_ref[rows, columns] = (part * cosine + swap_halves(part) * sine).astype(BF16)
        part = pre[:, qwidth : qwidth + LANES]
        part = part * cosine + swap_halves(part) * sine
        for ref, both in ((key_ref, part), (value_ref, values)):
            for kv, head in enumerate(split_heads(both)):
                ref[kv, rows, :] = jnp.where(extra, 1.0, head).astype(BF16)


def tables(packed):
    lane = lax.broadcasted_iota(jnp.int32, packed.shape, 1)
    turned = pltpu.roll(packed, HEAD_DIM, 1)
    low = lane < HEAD_DIM
    return jnp.where(low, packed, turned), jnp.where(low, turned, packed)


def attend_pair(pair, length, query_ref, key_ref, value_ref, mixed_ref, log_ref):
    scale = HEAD_DIM**-0.5
    columns = pl.ds(pl.multiple_of(pair * LANES, LANES), LANES)
    heads = [part.astype(BF16) for part in split_heads(query_ref[:, columns])]
    lane = lax.broadcasted_iota(jnp.int32, (BLOCK, LANES), 1)
    row = lax.broadcasted_iota(jnp.int32, (BLOCK, BLOCK), 0)
    col = lax.broadcasted_iota(jnp.int32, (BLOCK, BLOCK), 1)
    for index in range(length // BLOCK):
        rows = slice(index * BLOCK, (index + 1) * BLOCK)
        seen = index * BLOCK
        outs = []
        for which in range(2):
            head = 2 * pair + which
            kv = head // GROUP
            query = heads[which][rows]
            diagonal = mm(query, key_ref[kv, rows, :], NT) * scale
            diagonal = jnp.where(row >= col, diagonal, -1e30)
            top = jnp.max(diagonal, axis=-1, keepdims=True)
            if seen:
                before = mm(query, key_ref[kv, :seen, :], NT) * scale
                top = jnp.maximum(top, jnp.max(before, axis=-1, keepdims=True))
            probs = jnp.exp(diagonal - top).astype(BF16)
            mixed = mm(probs, value_ref[kv, rows, :])
            if seen:
                probs = jnp.exp(before - top).astype(BF16)
                mixed = mixed + mm(probs, value_ref[kv, :seen, :])
            total = mixed[:, HEAD_DIM : HEAD_DIM + 1]
            outs.append(mixed / total)
            log_ref[rows, :] = jnp.where(lane == head, top + jnp.log(total), log_ref[rows, :])
        mixed_ref[rows, columns] = join_heads(outs[0], outs[1]).astype(BF16)


def settle(length, x_ref, mixed_ref, weight_ref, vectors_ref, hidden_ref, normed_ref, turned_ref):
    width = x_ref.shape[2]
    gain = vectors_ref[2:3, :width]
    weight = weight_ref[1, :, :, BOTH - width :].reshape(width, width)
    for index in range(length // BLOCK):
        rows = slice(index * BLOCK, (index + 1) * BLOCK)
        half, start = index * BLOCK // (length // 2), index * BLOCK % (length // 2)
        hidden = x_ref[half, start : start + BLOCK, :].astype(F32) + mm(mixed_ref[rows, :], weight)
        hidden_ref[rows, :] = hidden
        scale = lax.rsqrt(jnp.mean(hidden * hidden, axis=-1, keepdims=True) + EPS)
        normed = (hidden * scale * gain).astype(BF16)
        normed_ref[rows, :] = normed
        turned_ref[:, rows] = normed.T


HALVES = ((0, 1), (2, 3))
WAYS = ((1, CHIPS // 2), (-1, CHIPS - 1 - CHIPS // 2))


def row_cuts(rows):
    early = rows // 2 // 16 * 16 if rows == 112 else 80
    return (0, early), (early, rows - early)


def feed_gather(ring, own_wide, own_down, wide, down, sems):
    rows, count = own_wide.shape[1], own_down.shape[0]
    pieces = []
    for (start, some), (down_start, down_some) in zip(row_cuts(rows), row_cuts(count)):

        def down_block(chip, start=down_start, some=down_some):
            return down.at[pl.ds(pl.multiple_of(chip * count + start, 16), some), :]

        def wide_block(chip, start=start, some=some):
            return wide.at[ring.mine, chip, pl.ds(start, some), :]

        pieces.append((1, own_down.at[pl.ds(down_start, down_some), :], down_block, None, 0, CHIPS - 1))
        pieces.append((-1, own_wide.at[ring.mine, pl.ds(start, some), :], wide_block, ring.peer, 1, CHIPS - 1))
    return Gather(ring, pieces, sems)


def feed_keep(ring, own_wide, own_down, wide, down, sems):
    count = own_down.shape[0]
    rows = pl.ds(pl.multiple_of(ring.chip * count, 16), count)
    return [
        pltpu.make_async_copy(own_wide, wide.at[:, ring.chip], sems.at[0]),
        pltpu.make_async_copy(own_down, down.at[rows, :], sems.at[1]),
    ]


def feed_reduce(ring, wide, down, wide_part, down_part, scratch):
    rows, count = wide_part.shape[0], down_part.shape[0]
    pieces = []
    for (start, some), (down_start, down_some) in zip(row_cuts(rows), row_cuts(count)):

        def down_block(chip, start=down_start, some=down_some):
            return down.at[pl.ds(pl.multiple_of(chip * count + start, 16), some), :]

        def own_block(chip, start=start, some=some):
            return wide.at[ring.mine, chip, pl.ds(start, some), :]

        def other_block(chip, start=start, some=some):
            return wide.at[1 - ring.mine, chip, pl.ds(start, some), :]

        down_out = down_part.at[pl.ds(down_start, down_some), :]
        pieces.append((1, down_block, None, None, down_out, CHIPS - 1, True))
        pieces.append((
            -1, own_block, other_block, ring.peer, wide_part.at[pl.ds(start, some), :], CHIPS - 1, True
        ))
    return make_reduce(ring, pieces, scratch)


def feed_reduce_scratch(rows, span, count, width):
    shapes = []
    for (_, some), (_, down_some) in zip(row_cuts(rows), row_cuts(count)):
        shapes += [(down_some, width, False), (some, span, True)]
    return reduce_scratch(shapes)


def first_kernel(
    length, plan,
    x_in, table_in, both_in, small_in, gate_in, up_in, down_in, cot_in,
    x_out, table_out, weight_out, turned1_out, query_out, key_out, value_out,
    vectors_ref, mixed_ref, log_ref, hidden_ref, own_wide2, own_down2,
    cot_out, wide_out, down_out, normed_out, turned_out,
    x_ref, table_ref, weight_ref, turned1_ref, query_ref, key_ref, value_ref,
    normed_ref, turned_ref, both_land, small_land, both_own, small_own, small_all, perm_ref, wide_land, own_wide1, own_down1,
    swap_sems, core_sems, keep_sems, cot_sems, store_sems, *sems,
):
    step = pl.program_id(0)
    ring = Ring(CHIPS)
    core, mine = ring.core, ring.mine
    gather = feed_gather(ring, own_wide1, own_down1, wide_out, down_out, sems[:4])
    keeps = feed_keep(ring, own_wide1, own_down1, wide_out, down_out, keep_sems)
    early = BOTH // 2
    pieces = []
    for start in (0, early):
        part = pl.ds(start, early)
        for direction, reach in WAYS:
            pieces.append((
                direction, both_own.at[:, part], lambda chip, part=part: weight_ref.at[core, chip, :, part],
                ring.partner, 0 if direction > 0 else 1, reach,
            ))
    for direction, reach in WAYS:
        pieces.append((direction, small_own, lambda chip: small_all.at[chip], None, 0, reach))
    attention = Gather(ring, pieces, sems[4:])
    every = range(len(pieces))
    swaps = [
        remote(src.at[1 - mine], dst.at[mine], swap_sems.at[2 * k], swap_sems.at[2 * k + 1], ring.peer)
        for k, (src, dst) in enumerate([(x_in, x_ref), (table_in, table_ref), (cot_in, cot_out.at[core])])
    ]
    trades = [
        remote(src, dst, core_sems.at[2 * k], core_sems.at[2 * k + 1], ring.partner)
        for k, (src, dst) in enumerate([
            (both_in.at[1 - core], both_land), (small_in, small_land), (perm_ref.at[1 - core], wide_land),
            (cot_out.at[core], cot_out.at[core]), (normed_ref, normed_out.at[core]),
            (turned_ref, turned_out.at[core]),
        ])
    ]
    cot_keep = pltpu.make_async_copy(cot_in.at[mine], cot_out.at[core, mine], cot_sems.at[0])
    stores = [
        pltpu.make_async_copy(src, dst, store_sems.at[k])
        for k, (src, dst) in enumerate([
            (x_ref, x_out), (table_ref, table_out), (weight_ref, weight_out), (turned1_ref, turned1_out),
            (query_ref, query_out), (key_ref, key_out), (value_ref, value_out),
            (normed_ref, normed_out.at[core]), (turned_ref, turned_out.at[core]),
        ])
    ]

    @pl.when(step == 0)
    def enter():
        ring.greet([ring.right, ring.left, ring.partner, ring.peer])
        trades[0].start()
        trades[1].start()
        for swap in swaps:
            swap.start()
        cot_keep.start()
        x_ref[mine] = x_in[mine]
        table_ref[mine] = table_in[mine]
        trades[0].wait()
        trades[1].wait()
        half = small_in.shape[0]
        rows = both_in.shape[1]
        for which in range(2):

            @pl.when(core == which)
            def own(which=which):
                pair = (both_in[which], both_land[...])
                both_own[...] = stack_rows(*pair[:: 1 - 2 * which]).astype(BF16)
                pair = (small_in[...], small_land[...])[:: 1 - 2 * which]
                lane = lax.broadcasted_iota(jnp.int32, (2 * half, LANES), 1)
                gains = stack_rows(pair[0][:rows], pair[1][:rows])
                gains = jnp.concatenate([gains, jnp.zeros((2 * (half - rows), LANES), F32)], axis=0)
                small_own[...] = jnp.where(lane == 0, stack_rows(*pair), gains).astype(BF16)

        attention.advance(0, every)
        weight_ref[core, ring.chip] = both_own[...]
        small_all[ring.chip] = small_own[...]
        wide = stack_rows(gate_in[...], up_in[...]).astype(BF16)
        for side in range(2):
            for group, span in enumerate(spans()):

                def store(tile, part, side=side, first=group * spans()[0]):
                    columns = slice(first + tile * LANES, first + (tile + 1) * LANES)
                    perm_ref[side, 0, :, columns] = part[:rows].astype(BF16)
                    perm_ref[side, 1, :, columns] = part[rows:].astype(BF16)

                gather_columns(wide, side, group, store)
        trades[2].start()
        own = sum(SPLITS)
        for group, ref in enumerate((own_down1, own_down2)):
            start, count = STARTS[group], SPLITS[group]
            ref[...] = stack_rows(
                down_in[start : start + count, :], down_in[own + start : own + start + count, :]
            ).astype(BF16)
        attention.advance(1, every)
        trades[2].wait()
        for which in range(2):

            @pl.when(core == which)
            def chip_rows(which=which):
                for tensor in range(2):
                    pair = (perm_ref[which, tensor], wide_land[tensor])
                    block = stack_rows(*pair[:: 1 - 2 * which]).astype(BF16)
                    own_wide1[tensor] = block[:, : spans()[0]]
                    own_wide2[tensor] = block[:, spans()[0] :]

        gather.advance(0, (0, 1, 2, 3))
        for keep in keeps:
            keep.start()
        for hop in range(2, WAYS[0][1] + 1):
            attention.advance(hop, every)
            if hop == 3:
                gather.advance(1, HALVES[0])
        gather.advance(1, HALVES[1])
        attention.finish()
        rows = small_all.shape[1]
        turned = small_all[...].astype(F32).reshape(CHIPS * rows, LANES).T
        vectors_ref[0:1, :] = turned[0:1, :]
        width = x_in.shape[2]
        chip_rows = width // CHIPS
        turned = small_all[:, :chip_rows, :].astype(F32).reshape(width, LANES).T
        vectors_ref[1:3, :width] = turned[1:3, :]
        swaps[0].wait()
        swaps[1].wait()
        project(length, x_ref, table_ref, vectors_ref, weight_ref, turned1_ref, query_ref, key_ref, value_ref)
        for store in stores[:-2]:
            store.start()
        log_ref[...] = jnp.zeros_like(log_ref)

    at_point(step, 1, plan, 1, 0, gather)

    @pl.when((step >= 1) & (step <= PAIRS))
    def pairs():
        attend_pair(step - 1, length, query_ref, key_ref, value_ref, mixed_ref, log_ref)

    @pl.when(step == 4)
    def cotangent():
        swaps[2].wait()
        cot_keep.wait()
        trades[3].start()

    @pl.when(step == PAIRS + 1)
    def last():
        settle(length, x_ref, mixed_ref, weight_ref, vectors_ref, hidden_ref, normed_ref, turned_ref)
        for copy in trades[4:] + stores[-2:]:
            copy.start()
        at_end(plan, gather)
        for copy in keeps + trades[3:] + stores:
            copy.wait()


def first_part(x, table, both, small, gate, up, down, cot):
    _, half, width = x.shape
    tokens = 2 * half
    rows, ff = gate.shape
    one, two = spans()
    down_rows = [2 * split for split in SPLITS]
    stored = [
        (x.shape, BF16), (table.shape, F32), ((2, CHIPS, 2 * rows, BOTH), BF16), ((width, tokens), BF16),
        ((tokens, width), BF16), ((KV_HEADS, tokens, LANES), BF16), ((KV_HEADS, tokens, LANES), BF16),
    ]
    kept = [
        ((8, 2 * CHIPS * small.shape[0]), F32), ((tokens, width), BF16), ((tokens, LANES), F32),
        ((tokens, width), F32),
        ((2, 2 * rows, two), BF16), ((down_rows[1], width), BF16),
    ]
    far = [
        ((2,) + cot.shape, BF16), ((2, CHIPS, 2 * rows, one), BF16), ((CHIPS * down_rows[0], width), BF16),
        ((2, tokens, width), BF16), ((2, width, tokens), BF16),
    ]
    ins = [x, table, both, small, gate, up, down]
    steps = [(hop, half) for hop in range(2, CHIPS) for half in HALVES]
    points = PAIRS + 1
    plan = [[] for _ in range(points + 1)]
    for index, move in enumerate(steps):
        plan[-(-(index + 1) * points // len(steps))].append(move)
    return pl.pallas_call(
        functools.partial(first_kernel, tokens, plan),
        grid=(PAIRS + 2,),
        in_specs=[inside(part.shape) for part in ins] + [ANY],
        out_specs=[ANY] * len(stored) + [inside(shape) for shape, _ in kept] + [ANY] * len(far),
        out_shape=[jax.ShapeDtypeStruct(shape, kind) for shape, kind in stored + kept + far],
        scratch_shapes=[pltpu.VMEM(shape, kind) for shape, kind in stored]
        + [
            pltpu.VMEM((tokens, width), BF16), pltpu.VMEM((width, tokens), BF16),
            pltpu.VMEM(both.shape[1:], BF16), pltpu.VMEM(small.shape, BF16),
            pltpu.VMEM((2 * rows, BOTH), BF16), pltpu.VMEM((2 * small.shape[0], LANES), BF16),
            pltpu.VMEM((CHIPS, 2 * small.shape[0], LANES), BF16),
            pltpu.VMEM((2, 2, rows, one + two), BF16), pltpu.VMEM((2, rows, one + two), BF16),
            pltpu.VMEM((2, 2 * rows, one), BF16), pltpu.VMEM((down_rows[0], width), BF16),
            dma(6), dma(12), dma(2), dma(1), dma(len(stored) + 2),
        ]
        + gather_sems(4)
        + gather_sems(6),
        compiler_params=pltpu.CompilerParams(
            collective_id=0, has_side_effects=True, vmem_limit_bytes=VMEM_LIMIT
        ),
    )(*ins, cot)


def feed_chunk(count, offset, normed_ref, turned_ref, cot_ref, wide, down, result_ref, d_normed_ref, work, pause):
    width = normed_ref.shape[2]
    columns = pl.ds(offset, count)
    gate_weight = wide[0, :, :, columns].reshape(width, count)
    up_weight = wide[1, :, :, columns].reshape(width, count)
    down_weight = down[columns, :]
    act_at, gate_at, up_at = (slice(k * CHUNK, k * CHUNK + count) for k in range(3))
    parts = normed_ref.shape[1] // QUARTER
    for part in range(2 * parts):
        core, rows = part // parts, slice(part % parts * QUARTER, (part % parts + 1) * QUARTER)
        normed, cot = normed_ref[core, rows, :], cot_ref[core, rows, :]
        gate = mm(normed, gate_weight)
        up = mm(normed, up_weight)
        d_act = mm(cot, down_weight, NT)
        sigma = jax.nn.sigmoid(gate)
        silu = gate * sigma
        act = (silu * up).astype(BF16)
        d_gate = (d_act * up * sigma * (1.0 + gate * (1.0 - sigma))).astype(BF16)
        d_up = (d_act * silu).astype(BF16)
        work[core, rows, act_at], work[core, rows, gate_at], work[core, rows, up_at] = act, d_gate, d_up
        result_ref[core, rows, :] += mm(act, down_weight)
        d_normed_ref[core, rows, :] += mm(d_gate, gate_weight, NT) + mm(d_up, up_weight, NT)
        if part + 1 == parts:
            pause(1)
    pause(2)
    for tensor, at in ((0, gate_at), (1, up_at)):
        grad = mm(turned_ref[0], work[0, :, at]) + mm(turned_ref[1], work[1, :, at])
        wide[tensor, :, :, columns] = grad.astype(BF16).reshape(wide.shape[1], wide.shape[2], count)
    grad = mm(work[0, :, act_at], cot_ref[0], TN) + mm(work[1, :, act_at], cot_ref[1], TN)
    down[columns, :] = grad.astype(BF16)


def feed_kernel(
    gather_plan, reduce_plan,
    normed_ref, turned_ref, cot_ref, hidden_in, wide_in, down_in, own_wide, own_down,
    result_out, d_normed_out, other_out, wide_out, down_out, wide_part, down_part,
    result_ref, d_normed_ref, work, wide1, down1, wide2, down2,
    load_sems, keep_sems, trade_sems, store_sems, *scratch,
):
    step = pl.program_id(0)
    ring = Ring(CHIPS)
    core = ring.core
    gather = feed_gather(ring, own_wide, own_down, wide2, down2, scratch[:4])
    keeps = feed_keep(ring, own_wide, own_down, wide2, down2, keep_sems)
    reduce = feed_reduce(ring, wide1, down1, wide_part, down_part, scratch[4:])
    loads = [
        pltpu.make_async_copy(src, dst, load_sems.at[k])
        for k, (src, dst) in enumerate([(wide_in, wide1), (down_in, down1), (hidden_in, result_ref.at[core])])
    ]
    trades = [
        remote(work.at[k], other_out.at[k], trade_sems.at[2 * k], trade_sems.at[2 * k + 1], ring.partner)
        for k in range(2)
    ]
    stores = [
        pltpu.make_async_copy(src, dst, store_sems.at[k])
        for k, (src, dst) in enumerate([
            (wide2, wide_out), (down2, down_out), (result_ref.at[core], result_out),
            (d_normed_ref.at[core], d_normed_out),
        ])
    ]
    one, two = wide1.shape[3], wide2.shape[3]
    turns, last = one // CHUNK, one // CHUNK + -(-two // CHUNK) - 1

    @pl.when(step == 0)
    def begin():
        for load in loads:
            load.start()
        ring.greet([ring.right, ring.left, ring.partner, ring.peer])

    at_point(step, 0, gather_plan, 3, 0, gather)

    @pl.when(step == 0)
    def start():
        for keep in keeps:
            keep.start()
        result_ref[1 - core] = jnp.zeros(result_ref.shape[1:], F32)
        d_normed_ref[...] = jnp.zeros_like(d_normed_ref)
        for load in loads:
            load.wait()

    def chunk(count, offset, wide, down, first, plan, transfer):
        feed_chunk(
            count, offset, normed_ref, turned_ref, cot_ref, wide, down, result_ref, d_normed_ref, work,
            lambda which: at_point(step, first, plan, 3, which, transfer),
        )

    @pl.when(step < turns)
    def first_group():
        chunk(CHUNK, pl.multiple_of(step * CHUNK, CHUNK), wide1, down1, 0, gather_plan, gather)

    @pl.when(step == turns - 1)
    def between():
        at_end(gather_plan, gather)
        for keep in keeps:
            keep.wait()
        reduce.begin()

    at_point(step, turns, reduce_plan, 3, 0, reduce)

    @pl.when((step >= turns) & (step < last))
    def second_group():
        chunk(CHUNK, pl.multiple_of((step - turns) * CHUNK, CHUNK), wide2, down2, turns, reduce_plan, reduce)

    @pl.when(step == last)
    def end():
        done = (last - turns) * CHUNK
        chunk(two - done, done, wide2, down2, turns, reduce_plan, reduce)
        for store in stores:
            store.start()
        work[0] = result_ref[1 - core].astype(BF16)
        trades[0].start()
        work[1] = d_normed_ref[1 - core].astype(BF16)
        trades[1].start()
        at_end(reduce_plan, reduce)
        for copy in trades + stores:
            copy.wait()


def feed(normed, turned, cot, hidden, wide, down, own_wide, own_down):
    _, tokens, width = normed.shape
    one, two = wide.shape[3], own_wide.shape[2]
    rows = own_wide.shape[1]
    counts = [2 * split for split in SPLITS]
    turns, more = one // CHUNK, -(-two // CHUNK)
    wide_two, down_two = (2, CHIPS, rows, two), (CHIPS * counts[1], width)
    whole, halves = (tokens, width), (2, tokens, width)
    far = [(whole, F32), (whole, F32), (halves, BF16), (wide_two, BF16), (down_two, BF16)]
    near = [((rows, one), F32), ((counts[0], width), F32)]
    return pl.pallas_call(
        functools.partial(
            feed_kernel, spread(3 * turns, HALVES, len(HALVES)), spread(3 * more, HALVES, 0)
        ),
        grid=(turns + more,),
        in_specs=[inside(part.shape) for part in (normed, turned, cot)] + [ANY] * 5,
        out_specs=[ANY] * len(far) + [inside(shape) for shape, _ in near],
        out_shape=[jax.ShapeDtypeStruct(shape, kind) for shape, kind in far + near],
        scratch_shapes=[
            pltpu.VMEM(halves, F32), pltpu.VMEM(halves, F32), pltpu.VMEM(halves, BF16),
            pltpu.VMEM(wide.shape, BF16), pltpu.VMEM(down.shape, BF16),
            pltpu.VMEM(wide_two, BF16), pltpu.VMEM(down_two, BF16),
            dma(3), dma(2), dma(4), dma(4),
        ]
        + gather_sems(4)
        + feed_reduce_scratch(rows, one, counts[0], width),
        compiler_params=pltpu.CompilerParams(
            collective_id=1, has_side_effects=True, vmem_limit_bytes=VMEM_LIMIT
        ),
    )(normed, turned, cot, hidden, wide, down, own_wide, own_down)


def unsettle(
    rows, first, hidden_ref, d_own_ref, other_ref, own_ref, cot_ref, vectors_ref, mixed_ref, weight_ref,
    d_hidden_ref, d_mixed_ref, output_grad_ref, second_ref, result_ref, place,
):
    width = hidden_ref.shape[1]
    gain = vectors_ref[2:3, :width]
    weight = weight_ref[0, :, BOTH - width :]
    hidden = hidden_ref[...]
    upstream = d_own_ref[...] + other_ref[1].astype(F32)
    scale = lax.rsqrt(jnp.mean(hidden * hidden, axis=-1, keepdims=True) + EPS)
    weighted = upstream * gain
    inner = jnp.mean(weighted * hidden, axis=-1, keepdims=True)
    d_hidden = cot_ref[rows, :].astype(F32) + scale * weighted - hidden * (scale * scale * scale * inner)
    d_hidden_ref[rows, :] = d_hidden
    result_ref[place] = (own_ref[...] + other_ref[0].astype(F32)).astype(BF16)
    branch = d_hidden.astype(BF16)
    d_mixed_ref[rows, :] = mm(branch, weight, NT).astype(BF16)
    grad = mm(mixed_ref[rows, :], branch, TN)
    part = jnp.sum(upstream * hidden * scale, axis=0, keepdims=True)

    @pl.when(first)
    def begin():
        second_ref[...] = part
        output_grad_ref[...] = grad

    @pl.when(jnp.logical_not(first))
    def more():
        second_ref[...] += part
        output_grad_ref[...] += grad


def back_head(pair, which, length, query_ref, grad_ref, mixed_ref, log_ref, key_ref, value_ref, d_key_ref, d_value_ref):
    scale = HEAD_DIM**-0.5
    columns = pl.ds(pl.multiple_of(pair * LANES, LANES), LANES)
    query, grad, mixed = (split_heads(ref[:, columns])[which] for ref in (query_ref, grad_ref, mixed_ref))
    lane = lax.broadcasted_iota(jnp.int32, (length, LANES), 1)
    row = lax.broadcasted_iota(jnp.int32, (BLOCK, BLOCK), 0)
    col = lax.broadcasted_iota(jnp.int32, (BLOCK, BLOCK), 1)
    head = 2 * pair + which
    kv = head // GROUP
    log_total = jnp.sum(jnp.where(lane == head, log_ref[...], 0.0), axis=-1, keepdims=True)
    inner = jnp.sum(grad * mixed, axis=-1, keepdims=True)
    query_low, grad_low = query.astype(BF16), grad.astype(BF16)
    query, grad = widen(query * scale, -log_total), widen(grad, -inner)
    parts = [None] * (length // BLOCK)
    for index in range(length // BLOCK):
        own = slice(index * BLOCK, (index + 1) * BLOCK)
        keys, values = key_ref[kv, own, :], value_ref[kv, own, :]
        key_sum = value_sum = None
        for other in range(index, length // BLOCK):
            rows = slice(other * BLOCK, (other + 1) * BLOCK)
            scores = mm(keys, query[rows], NT)
            if other == index:
                scores = jnp.where(row <= col, scores, -1e30)
            probs = jnp.exp(scores)
            d_scores = (probs * mm(values, grad[rows], NT)).astype(BF16)
            value_part = mm(probs.astype(BF16), grad_low[rows])
            key_part = mm(d_scores, query_low[rows])
            key_sum = key_part if key_sum is None else key_sum + key_part
            value_sum = value_part if value_sum is None else value_sum + value_part
            part = mm(d_scores, keys, TN)
            parts[other] = part if parts[other] is None else parts[other] + part
        d_key_ref[kv, own, :] += key_sum * scale
        d_value_ref[kv, own, :] += value_sum
    return parts


def back_kernel_all(
    length, plan,
    hidden_ref, d_own_ref, other_ref, own_ref,
    vectors_ref, weight_ref, mixed_ref, query_ref, log_ref, key_ref, value_ref, wide_before, down_before,
    wide_ref, down_ref, cot_in,
    d_hidden_ref, output_grad_out, second_ref, d_query_ref, d_key_ref, d_value_ref,
    wide_own, down_own, wide_part, down_part, result_ref,
    d_mixed_ref, cot_ref, output_grad_ref, half_ref, load_sem, *scratch,
):
    step = pl.program_id(0)
    ring = Ring(CHIPS)
    share = Share(ring, wide_before, wide_own, scratch[:5])
    share_rows = ShareRows(ring, down_before, down_own, scratch[5:8])
    reduce = feed_reduce(ring, wide_ref, down_ref, wide_part, down_part, scratch[8:])
    load = pltpu.make_async_copy(cot_in.at[ring.core], cot_ref, load_sem.at[0])
    blocks = length // BLOCK

    @pl.when(step == 0)
    def begin():
        load.start()
        ring.greet([ring.right, ring.left, ring.partner, ring.peer])
        reduce.begin()
        share.first()
        share_rows.first()
        d_key_ref[...] = jnp.zeros_like(d_key_ref)
        d_value_ref[...] = jnp.zeros_like(d_value_ref)
        load.wait()

    at_point(step, 0, plan, 2, 0, reduce)

    @pl.when(step < blocks)
    def norms():
        rows = pl.ds(pl.multiple_of(step * BLOCK, BLOCK), BLOCK)
        halves = length // 2 // BLOCK
        place = (lax.div(step, halves), pl.ds(pl.multiple_of(lax.rem(step, halves) * BLOCK, BLOCK), BLOCK))
        unsettle(
            rows, step == 0, hidden_ref, d_own_ref, other_ref, own_ref, cot_ref, vectors_ref, mixed_ref, weight_ref,
            d_hidden_ref, d_mixed_ref, output_grad_ref, second_ref, result_ref, place,
        )

    @pl.when(step == blocks - 1)
    def after():
        output_grad_out[...] = output_grad_ref[...].astype(BF16)
        share.second()
        share_rows.second()

    refs = (query_ref, d_mixed_ref, mixed_ref, log_ref, key_ref, value_ref, d_key_ref, d_value_ref)

    @pl.when(step >= blocks)
    def first_head():
        parts = back_head(step - blocks, 0, length, *refs)
        for index, part in enumerate(parts):
            half_ref[index * BLOCK : (index + 1) * BLOCK, :] = part

    at_point(step, 0, plan, 2, 1, reduce)

    @pl.when(step >= blocks)
    def second_head():
        scale = HEAD_DIM**-0.5
        columns = pl.ds(pl.multiple_of((step - blocks) * LANES, LANES), LANES)
        parts = back_head(step - blocks, 1, length, *refs)
        for index, part in enumerate(parts):
            rows = slice(index * BLOCK, (index + 1) * BLOCK)
            d_query_ref[rows, columns] = (join_heads(half_ref[rows, :], part) * scale).astype(BF16)

    @pl.when(step == blocks + PAIRS - 1)
    def last():
        at_end(plan, reduce)
        share.third()


def back_all(
    hidden, d_own, other, own, vectors, weight, mixed, query, logs, keys, values, wide_before, down_before,
    wide, down, cot,
):
    tokens, width = hidden.shape
    rows, before = wide_before.shape
    span = wide.shape[3]
    counts = [2 * split for split in SPLITS]
    blocks = tokens // BLOCK

    def block(step):
        return jnp.minimum(step, blocks - 1)

    line = pl.BlockSpec((BLOCK, width), lambda s: (block(s), 0))
    pair = pl.BlockSpec((2, BLOCK, width), lambda s: (0, block(s), 0))
    late = pl.BlockSpec((1, width, BOTH), lambda s: (1, 0, 0), pipeline_mode=pl.Buffered(1))
    ins = [mixed, query, logs, keys, values, wide_before, down_before, wide, down]
    outs = [
        ((tokens, width), F32), ((width, width), BF16), ((1, width), F32), (query.shape, BF16),
        (keys.shape, F32), (values.shape, F32),
        ((2, 2, rows // OWNERS, before), F32), ((counts[0] // 2, width), F32),
        ((rows, span), F32), ((counts[1], width), F32), ((2, tokens // 2, width), BF16),
    ]
    moves = [(hop, half) for hop in range(CHIPS) for half in HALVES]
    plan = [[] for _ in range(2 * (blocks + PAIRS) + 1)]
    for place, move in zip([2 * blocks - 4, 2 * blocks - 2] + list(range(2 * blocks, len(plan) - 1)), moves):
        plan[place].append(move)
    return pl.pallas_call(
        functools.partial(back_kernel_all, tokens, plan),
        grid=(blocks + PAIRS,),
        in_specs=[line, line, pair, line, inside(vectors.shape), late]
        + [inside(part.shape) for part in ins]
        + [ANY],
        out_specs=[inside(shape) for shape, _ in outs],
        out_shape=[jax.ShapeDtypeStruct(shape, kind) for shape, kind in outs],
        scratch_shapes=[
            pltpu.VMEM((tokens, width), BF16), pltpu.VMEM((tokens, width), BF16),
            pltpu.VMEM((width, width), F32), pltpu.VMEM((tokens, LANES), F32), dma(1),
        ]
        + share_scratch(rows // OWNERS, before, True)
        + share_rows_scratch(counts[0] // 2, width)
        + feed_reduce_scratch(rows, span, counts[1], width),
        compiler_params=pltpu.CompilerParams(
            collective_id=2, has_side_effects=True, vmem_limit_bytes=VMEM_LIMIT
        ),
    )(hidden, d_own, other, own, vectors, weight, *ins, cot)


def last_kernel(
    length,
    d_query_ref, d_key_ref, d_value_ref, table_ref, turned_ref, x_ref, vectors_ref, weight_ref, d_hidden_ref,
    output_grad_ref, second_ref, wide_first, down_first, wide_before, down_before, result_ref,
    qkv_grad_out, output_grad_out, bits_out, gate_grad_out, up_grad_out, down_grad_out, input_grad_out, result_out,
    d_pre_ref, both_ref, part_ref, both_own, wide_own, down_own, bits_ref, bits_land, bits_sum,
    input_grad_ref, input_grad_land, bits_send, bits_recv, swap_sems, bit_sems, *scratch,
):
    ring = Ring(CHIPS)
    core, mine = ring.core, ring.mine
    others = [{"fsdp": 2 * ring.chip_at(offset) + core} for offset in range(1, CHIPS)]
    ring.greet(others + [ring.partner, ring.peer])
    share = Share(ring, wide_before, wide_own, scratch[:5])
    share_rows = ShareRows(ring, down_before, down_own, scratch[5:8])
    share_both = Share(ring, part_ref, both_own, scratch[8:13])
    early = BOTH // 2
    pieces = []
    for start in (0, early):
        part = pl.ds(start, early)
        for direction, reach in WAYS:
            pieces.append((
                direction,
                lambda chip, part=part: both_ref.at[core, chip, :, part],
                lambda chip, part=part: both_ref.at[1 - core, chip, :, part],
                ring.partner, part_ref.at[:, part], reach, direction > 0,
            ))
    reduce = make_reduce(ring, pieces, scratch[13:])
    share.first()
    share_rows.first()
    result_keep = pltpu.make_async_copy(result_ref.at[mine], result_out.at[mine], swap_sems.at[4])
    result_swap = remote(result_ref.at[1 - mine], result_out.at[mine], swap_sems.at[2], swap_sems.at[3], ring.peer)

    qwidth = HEADS * HEAD_DIM
    width = d_hidden_ref.shape[1]
    half = length // 2
    bias = None
    for index in range(length // BLOCK):
        rows = slice(index * BLOCK, (index + 1) * BLOCK)
        cosine, sine = tables(table_ref[index * BLOCK // half, index * BLOCK % half : index * BLOCK % half + BLOCK, :])

        def back(part):
            return (part * cosine - swap_halves(part) * sine).astype(BF16)

        for tile in range(PAIRS):
            columns = slice(tile * LANES, (tile + 1) * LANES)
            d_pre_ref[rows, columns] = back(d_query_ref[rows, columns].astype(F32))
        keys = join_heads(d_key_ref[0, rows, :], d_key_ref[1, rows, :]).astype(BF16).astype(F32)
        d_pre_ref[rows, qwidth : qwidth + LANES] = back(keys)
        values = join_heads(d_value_ref[0, rows, :], d_value_ref[1, rows, :])
        d_pre_ref[rows, qwidth + LANES :] = values.astype(BF16)
        part = jnp.sum(d_pre_ref[rows, :].astype(F32), axis=0, keepdims=True)
        bias = part if bias is None else bias + part

    chip_rows = width // CHIPS
    grad = mm(turned_ref[...], d_pre_ref[...]).astype(BF16)
    rest = grad.shape[1] - BOTH
    for chip in range(CHIPS):
        rows = slice(chip * chip_rows, (chip + 1) * chip_rows)
        both_ref[0, chip] = grad[rows, :BOTH]
        both_ref[1, chip, :, :rest] = grad[rows, BOTH:]
        both_ref[1, chip, :, rest:] = output_grad_ref[rows, :]
    reduce.begin()
    reduce.advance(0, range(len(pieces)))
    result_keep.start()
    result_swap.start()
    share.second()
    share_rows.second()

    gain = vectors_ref[1:2, :width]
    weight_early, weight_late = weight_ref[0], weight_ref[1, :, : qwidth + 2 * LANES - BOTH]
    first = None
    for index in range(length // BLOCK):
        rows = slice(index * BLOCK, (index + 1) * BLOCK)
        which, start = index * BLOCK // half, index * BLOCK % half
        x = x_ref[which, start : start + BLOCK, :].astype(F32)
        upstream = mm(d_pre_ref[rows, :BOTH], weight_early, NT) + mm(d_pre_ref[rows, BOTH:], weight_late, NT)
        scale = lax.rsqrt(jnp.mean(x * x, axis=-1, keepdims=True) + EPS)
        weighted = upstream * gain
        inner = jnp.mean(weighted * x, axis=-1, keepdims=True)
        d_x = d_hidden_ref[rows, :] + scale * weighted - x * (scale * scale * scale * inner)
        part = jnp.sum(upstream * x * scale, axis=0, keepdims=True)
        first = part if first is None else first + part
        input_grad_ref[which, start : start + BLOCK, :] = d_x.astype(BF16)
        reduce.advance(index + 1, range(len(pieces)))
    swap = remote(input_grad_ref.at[1 - mine], input_grad_land, swap_sems.at[0], swap_sems.at[1], ring.peer)
    swap.start()

    bits_ref[...] = jnp.zeros_like(bits_ref)
    for chip in range(CHIPS):
        line = 0
        for values, each in ((bias, bias.shape[1] // CHIPS), (first, chip_rows), (second_ref[...], chip_rows)):
            for owner in range(OWNERS):
                count = each // OWNERS
                start = chip * each + owner * count
                bits_ref[chip, line : line + 1, :count] = values[:, start : start + count]
                line += 1
    copies = [
        remote(bits_ref.at[ring.chip_at(k + 1)], bits_land.at[k], bits_send.at[k], bits_recv.at[k], others[k])
        for k in range(CHIPS - 1)
    ]
    for copy in copies:
        copy.start()
    input_grad_out[mine] = input_grad_ref[mine].astype(F32)
    share.third()
    down_grad_out[: down_first.shape[0], :] = down_first[...]
    down_grad_out[down_first.shape[0] :, :] = down_own[...]
    own_rows = gate_grad_out.shape[0]
    sources = []
    for ref in (wide_first, wide_own):
        sources.append([stack_rows(ref[0, k], ref[1, k]).astype(BF16) for k in range(2)])

    def store(tile, part):
        columns = slice(tile * LANES, (tile + 1) * LANES)
        gate_grad_out[:, columns] = part[:own_rows]
        up_grad_out[:, columns] = part[own_rows:]

    spread_columns(sources, store, gate_grad_out.shape[1])
    share_both.first()
    total = bits_ref[ring.chip]
    for k, copy in enumerate(copies):
        copy.wait()
        total = total + bits_land[k]
    bits_sum[0] = total
    over_core = remote(bits_sum.at[0], bits_sum.at[1], bit_sems.at[0], bit_sems.at[1], ring.partner)
    over_core.start()
    over_core.wait()
    bits_sum[2] = bits_sum[0] + bits_sum[1]
    over_seq = remote(bits_sum.at[2], bits_sum.at[3], bit_sems.at[2], bit_sems.at[3], ring.peer)
    over_seq.start()
    swap.wait()
    input_grad_out[1 - mine] = input_grad_land[...].astype(F32)
    share_both.second()
    over_seq.wait()
    bits_out[...] = bits_sum[2] + bits_sum[3]
    share_both.third()
    rest = qkv_grad_out.shape[1] - BOTH
    qkv_grad_out[:, :BOTH] = both_own[0]
    qkv_grad_out[:, BOTH:] = both_own[1, :, :rest]
    output_grad_out[...] = both_own[1, :, rest:]
    reduce.finish()
    result_swap.wait()
    result_keep.wait()


def last_part(
    d_query, d_key, d_value, table, turned, x, vectors, weight, d_hidden, output_grad, second,
    wide_first, down_first, wide_before, down_before, result,
):
    tokens, width = d_hidden.shape
    ins = [
        d_query, d_key, d_value, table, turned, x, vectors, weight, d_hidden, output_grad, second,
        wide_first, down_first, wide_before, down_before,
    ]
    rows, span = wide_before.shape
    own_rows = rows // OWNERS
    own = sum(SPLITS)
    halves = (2, tokens // 2, width)
    qkv = vectors.shape[1]
    outs = [
        (own_rows, qkv), (own_rows, width), (BITS, LANES), (own_rows, 2 * CHIPS * 2 * own),
        (own_rows, 2 * CHIPS * 2 * own), (own, width), halves,
    ]
    return pl.pallas_call(
        functools.partial(last_kernel, tokens),
        in_specs=[pl.BlockSpec(memory_space=pltpu.VMEM)] * len(ins) + [ANY],
        out_specs=[pl.BlockSpec(memory_space=pltpu.VMEM)] * len(outs) + [ANY],
        out_shape=[jax.ShapeDtypeStruct(shape, F32) for shape in outs]
        + [jax.ShapeDtypeStruct(result.shape, BF16)],
        scratch_shapes=[
            pltpu.VMEM((tokens, qkv), BF16), pltpu.VMEM((2, CHIPS, rows, BOTH), BF16),
            pltpu.VMEM((rows, BOTH), F32), pltpu.VMEM((2, own_rows, BOTH), F32),
            pltpu.VMEM((2, 2, own_rows, span), F32), pltpu.VMEM((SPLITS[1], width), F32),
            pltpu.VMEM((CHIPS, BITS, LANES), F32), pltpu.VMEM((CHIPS - 1, BITS, LANES), F32),
            pltpu.VMEM((4, BITS, LANES), F32), pltpu.VMEM(halves, BF16), pltpu.VMEM(halves[1:], BF16),
            dma(CHIPS - 1), dma(CHIPS - 1), dma(5), dma(4),
        ]
        + share_scratch(own_rows, span, True)
        + share_rows_scratch(SPLITS[1], width)
        + share_scratch(own_rows, BOTH, False)
        + reduce_scratch([(rows, BOTH // 2, True)] * 4),
        compiler_params=pltpu.CompilerParams(
            collective_id=3, has_side_effects=True, vmem_limit_bytes=VMEM_LIMIT
        ),
    )(*ins, result)


def ring_shards(
    inputs, positions, qkv_weight, qkv_bias, output_weight, first_gain,
    gate_weight, up_weight, down_weight, second_gain, cotangent,
):
    _, half, width = inputs.shape
    tokens = 2 * half
    rows = gate_weight.shape[0]
    freqs = THETA ** (-jnp.arange(0, HEAD_DIM, 2).astype(F32) / HEAD_DIM)
    angles = positions.astype(F32)[..., None] * freqs
    cosine, sine = jnp.cos(angles), jnp.sin(angles)
    table = jnp.concatenate([cosine, cosine, -sine, sine], axis=-1)
    both = jnp.stack([
        qkv_weight[:, :BOTH], jnp.concatenate([qkv_weight[:, BOTH:], output_weight], axis=1),
    ])
    own_bias = qkv_bias.shape[0]
    pad = (0, own_bias - rows)
    small = jnp.stack([qkv_bias, jnp.pad(first_gain, pad), jnp.pad(second_gain, pad)], axis=1)
    small = jnp.pad(small, ((0, 0), (0, LANES - 3)))
    (
        x, table, weight, turned1, query, keys, values,
        vectors, mixed, logs, hidden, own_wide, own_down, cot, wide, down, normed2, turned2,
    ) = first_part(inputs, table, both, small, gate_weight, up_weight, down_weight, cotangent)
    weight = weight.reshape(2, width, BOTH)
    cot = cot.reshape(2, tokens, width)
    own, d_own, other, wide_second, down_second, wide_part_first, down_part_first = feed(
        normed2, turned2, cot, hidden, wide, down, own_wide, own_down
    )
    (
        d_hidden, output_grad, second, d_query, d_key, d_value,
        wide_first, down_first, wide_part_second, down_part_second, result,
    ) = back_all(
        hidden, d_own, other, own, vectors, weight, mixed, query, logs, keys, values,
        wide_part_first, down_part_first, wide_second, down_second, cot,
    )
    qkv_grad, output_grad, bits, gate_grad, up_grad, down_grad, input_grad, result = last_part(
        d_query, d_key, d_value, table, turned1, x, vectors, weight, d_hidden, output_grad, second,
        wide_first, down_first, wide_part_second, down_part_second, result,
    )
    owner = 2 * lax.rem(lax.axis_index("fsdp"), 2) + lax.axis_index("seq")

    def own_bits(which, count):
        return lax.dynamic_index_in_dim(bits, which * OWNERS + owner, 0, keepdims=False)[:count]

    return (
        result,
        input_grad,
        qkv_grad,
        own_bits(0, own_bias // 2),
        output_grad,
        own_bits(1, rows // 2),
        gate_grad,
        up_grad,
        down_grad,
        own_bits(2, rows // 2),
    )


def solution(mesh):
    tokens = P("fsdp", "seq", None)
    rows, row = P("fsdp", None), P("fsdp")
    grads, grad = P(("fsdp", "seq"), None), P(("fsdp", "seq"))
    ready = mesh.shape["fsdp"] == 2 * CHIPS and mesh.shape["seq"] == 2
    step = ring_shards if ready else plain_shards
    return jax.shard_map(
        step,
        mesh=mesh,
        in_specs=(tokens, P("fsdp", "seq"), rows, row, rows, row, rows, rows, rows, row, tokens),
        out_specs=(tokens, tokens, grads, grad, grads, grad, grads, grads, grads, grad),
        check_vma=False,
    )
```

time: 2060 us -> 428 us (0.21)
  blocking collectives: 1140 us -> 0 us
  Pallas kernels: 0 us -> 408 us
  matrix products: 380 us -> 0 us
  local copies, waits for them, and re-layouts: 192 us -> 11.7 us
  other arithmetic: 111 us -> 4.73 us
  starting transfers between devices: 103 us -> 0 us
  waiting for transfers between devices: 94.5 us -> 0 us
    unnamed x3 -> x0, blocking collectives: 1140 us -> none
    pallas_call x0 -> x4, Pallas kernels: none -> 408 us  [the longest x1 161 us: feed(): pl.pallas_call(functools.partial(feed_kernel, spread(3 * turns, HALVES, l...]
    dot_general x29 -> x0, matrix products: 380 us -> none  [the longest x4 76.6 us: masked_scores(): jnp.einsum('sicgd,sjcd->scgij', rows, key_full, preferred_element_type=jn...]
    unnamed x17 -> x0, starting transfers between devices: 81.4 us -> none
    unnamed x128 -> x29, local copies, waits for them, and re-layouts: 87.8 us -> 8.55 us
    all_to_all x6 -> x0, waiting for transfers between devices: 66.4 us -> none  [the longest x1 35.6 us: shards(): lax.all_to_all(d_query, 'seq', split_axis=1, concat_axis=2, tiled=True)]
    another operation x7 -> x3, other arithmetic: 54.5 us -> 0.74 us  [the longest x2 0.73 us: ring_shards(): jnp.stack([qkv_weight[:, :BOTH], jnp.concatenate([qkv_weight[:, BOTH:], o...]
    reduce_sum x4 -> x0, other arithmetic: 32.7 us -> none  [the longest x2 30.2 us: forward_block(): total = jnp.sum(expo, axis=-1, keepdims=True)]
  transfers between devices with their start and end apart: 28 -> 0, of which waited for: 6 -> 0; matrix products, arithmetic and copies ran while one was open for 80% -> 0% of each run, Pallas kernels for 0% -> 0%
where the time goes in v1:
time: 428 us; the launch traced here: 425 us
  Pallas kernels  408 us (95%)
  local copies, waits for them, and re-layouts  11.7 us (3%)
  other arithmetic  4.73 us (1%)
    pallas_call x1, Pallas kernels, feed(): pl.pallas_call(functools.partial(feed_kernel, spread(3 * turns, HALVES, l...  161 us
    pallas_call x1, Pallas kernels, first_part(): pl.pallas_call(functools.partial(first_kernel, tokens, plan), grid=(PAIRS...  92.8 us
    pallas_call x1, Pallas kernels, back_all(): pl.pallas_call(functools.partial(back_kernel_all, tokens, plan), grid=(bl...  87.5 us
    pallas_call x1, Pallas kernels, last_part(): pl.pallas_call(functools.partial(last_kernel, tokens), in_specs=[pl.Block...  65.9 us

profile of v1, /device:TPU:0, one launch (start us, length us, event | category | flops | bytes accessed | tf_op | source)
XLA Modules:
  0.0 425.0 jit_solution(457548734625534897)
XLA Ops:
  0.6 0.0 copy-start.5
  0.7 0.0 slice-start
  0.7 0.0 copy-start.7
  0.7 0.0 copy-start.10
  0.7 0.0 copy-start.9
  0.7 0.0 copy-start.8
  0.7 0.8 convert_element_type.15
  1.5 1.9 multiply_cosine_fusion
  3.4 1.3 pad_maximum_fusion.table_in
  4.7 0.0 copy-done.5
  4.7 0.0 slice-done
  4.7 0.0 copy-done.7
  4.7 0.7 pad_maximum_fusion.1.both_in
  5.4 0.0 copy-done.10
  5.4 0.0 copy-done.9
  5.5 0.0 copy-done.8
  5.5 0.1 copy.26
  5.6 0.6 pad.13.small_in
  6.2 92.8 %shard_map.186 = (bf16[2,512,896]{2,1,0:T(8,128)(2,1)}, f32[2,512,128]{2,1,0:T(8,128)}, bf16[2,8,112,1024]{3,2,1,0:T(8,128)(2,1)}, bf16[896,1024]{1,0:T(8,128)(2...) custom-call(bf16[2,512,896]{2,1,0:T(8,128)(2,1)} %x_in.1, ...), custom_call_target="tpu_custom_call" | custom-call | tf_op jit(solution)/shard_map/pallas_call | solution.py:1083
  99.1 161.4 %shard_map.187 = (f32[1024,896]{1,0:T(8,128)}, f32[1024,896]{1,0:T(8,128)}, bf16[2,1024,896]{2,1,0:T(8,128)(2,1)}, bf16[2,8,112,1408]{3,2,1,0:T(8,128)(2,1)}, bf...) custom-call(bf16[2,1024,896]{2,1,0:T(8,128)(2,1)} %get-tuple-element.55.normed_ref, ...), custom_call_target="tpu_custom_call" | custom-call | tf_op jit(solution)/shard_map/pallas_call | solution.py:1235
  260.4 87.5 %shard_map.188 = (f32[1024,896]{1,0:T(8,128)}, bf16[896,896]{1,0:T(8,128)(2,1)}, f32[1,896]{1,0:T(1,128)}, bf16[1024,896]{1,0:T(8,128)(2,1)}, f32[2,1024,128]{2,...) custom-call(f32[1024,896]{1,0:T(8,128)} %get-tuple-element.54.hidden, ...), custom_call_target="tpu_custom_call" | custom-call | tf_op jit(solution)/shard_map/pallas_call | solution.py:1422
  348.0 65.9 %shard_map.189 = (f32[28,1152]{1,0:T(8,128)}, f32[28,896]{1,0:T(8,128)}, f32[16,128]{1,0:T(8,128)}, f32[28,4864]{1,0:T(8,128)}, f32[28,4864]{1,0:T(8,128)}, /*in...) custom-call(bf16[1024,896]{1,0:T(8,128)(2,1)} %get-tuple-element.76.d_query_ref, ...), custom_call_target="tpu_custom_call" | custom-call | tf_op jit(solution)/shard_map/pallas_call | solution.py:1605
  413.8 0.0 copy-start
  413.9 0.8 constant_dynamic-slice_fusion
  414.7 0.5 slice_bitcast_fusion.1
  415.2 0.5 slice_bitcast_fusion.2
  415.7 0.5 slice_bitcast_fusion.3
  416.2 2.9 copy.34
  419.1 0.0 copy-done
  419.1 0.0 copy-start.4
  419.1 0.0 copy-start.6
  419.1 0.0 copy-start.2
  419.1 0.0 copy-start.1
  419.1 0.0 copy-start.3
  419.1 1.9 copy.35
  421.0 0.0 copy-done.4
  421.0 0.7 copy.36
  421.7 0.0 copy-done.6
  421.7 0.6 copy.37
  422.3 0.0 copy-done.2
  422.3 0.8 copy.38
  423.2 0.0 copy-done.1
  423.2 0.8 copy.39
  424.0 0.0 copy-done.3
  424.0 0.8 copy.40
  (4 shorter events, 0.0 us)
Async XLA Ops:
  0.6 4.1 copy-start.5
  0.7 4.0 slice-start
  0.7 4.0 copy-start.7
  0.7 4.8 %copy-start.10 = (bf16[56]{0:T(256)(128)(2,1)S(1)}, bf16[56]{0:T(256)(128)(2,1)}, u32[]{:S(2)}) copy-start(bf16[56]{0:T(256)(128)(2,1)} %param.16) | copy-start | bytes 340
  0.7 4.8 %copy-start.9 = (bf16[56]{0:T(256)(128)(2,1)S(1)}, bf16[56]{0:T(256)(128)(2,1)}, u32[]{:S(2)}) copy-start(bf16[56]{0:T(256)(128)(2,1)} %param.20) | copy-start | bytes 340
  0.7 4.8 %copy-start.8 = (bf16[72]{0:T(256)(128)(2,1)S(1)}, bf16[72]{0:T(256)(128)(2,1)}, u32[]{:S(2)}) copy-start(bf16[72]{0:T(256)(128)(2,1)} %param.14) | copy-start | bytes 436
  413.8 5.3 %copy-start = (f32[2,512,896]{2,1,0:T(8,128)S(1)}, f32[2,512,896]{2,1,0:T(8,128)}, u32[]{:S(2)}) copy-start(f32[2,512,896]{2,1,0:T(8,128)} %get-tuple-element.119) | copy-start | bytes 11010052
  419.1 1.9 copy-start.4
  419.1 2.6 copy-start.6
  419.1 3.2 copy-start.2
  419.1 4.0 copy-start.1
  419.1 4.9 %copy-start.3 = (f32[152,896]{1,0:T(8,128)S(1)}, f32[152,896]{1,0:T(8,128)}, u32[]{:S(2)}) copy-start(f32[152,896]{1,0:T(8,128)} %get-tuple-element.126) | copy-start | bytes 1634308

commit v2 on v1

--- a/solution.py
+++ b/solution.py
@@ -700,60 +700,24 @@
     return jnp.concatenate([first.astype(F32), second.astype(F32)], axis=0)
 
 
-def one_hot(rows, segments):
-    row = lax.broadcasted_iota(jnp.int32, (rows, LANES), 0)
-    col = lax.broadcasted_iota(jnp.int32, (rows, LANES), 1)
-    found = None
-    for a, b, shift in segments:
-        here = (row - col == shift) & (col >= a) & (col < b)
-        found = here if found is None else found | here
-    return jnp.where(found, 1.0, 0.0).astype(BF16)
-
-
-def owner_columns(core, group, section):
+def owner_columns(core, group):
     own = sum(SPLITS)
-    return (section // 2) * OWNERS * own + 2 * own * core + (section % 2) * own + STARTS[group]
-
-
-def gather_columns(source, core, group, store):
-    split = SPLITS[group]
-    for tile in range(2 * CHIPS * split // LANES):
-        segments, low, high = [], None, None
-        for section in range(tile * LANES // split, ((tile + 1) * LANES - 1) // split + 1):
-            a = max(section * split - tile * LANES, 0)
-            b = min((section + 1) * split - tile * LANES, LANES)
-            shift = owner_columns(core, group, section) + tile * LANES - section * split
-            segments.append((a, b, shift))
-            low = a + shift if low is None else low
-            high = b + shift
-        start = low // LANES * LANES
-        count = -(-(high - start) // LANES) * LANES
-        pick = one_hot(count, [(a, b, shift - start) for a, b, shift in segments])
-        store(tile, mm(source[:, start : start + count], pick))
-
-
-def spread_columns(sources, store, width):
-    own = sum(SPLITS)
-    for tile in range(width // LANES):
-        total = None
-        column = tile * LANES
-        while column < (tile + 1) * LANES:
-            chip, rest = divmod(column, OWNERS * own)
-            core, rest = divmod(rest, 2 * own)
-            seq, rest = divmod(rest, own)
-            group = 0 if rest < SPLITS[0] else 1
-            left = SPLITS[0] - rest if group == 0 else own - rest
-            stop = min(column + left, (tile + 1) * LANES)
-            index = (2 * chip + seq) * SPLITS[group] + rest - STARTS[group]
-            start = index // LANES * LANES
-            a, b = column - tile * LANES, stop - tile * LANES
-            high = index + b - a
-            count = -(-(high - start) // LANES) * LANES
-            pick = one_hot(count, [(a, b, index - a - start)])
-            part = mm(sources[group][core][:, start : start + count], pick)
-            total = part if total is None else total + part
-            column = stop
-        store(tile, total)
+    starts = [OWNERS * own * chip + 2 * own * core + own * seq for chip in range(CHIPS) for seq in range(2)]
+    return [(start + STARTS[group], SPLITS[group]) for start in starts]
+
+
+def gather_columns(source, core, group):
+    return jnp.concatenate([source[:, a : a + count] for a, count in owner_columns(core, group)], axis=1)
+
+
+def spread_columns(sources):
+    parts = []
+    for chip in range(CHIPS):
+        for core in range(2):
+            for section in range(2 * chip, 2 * chip + 2):
+                for group, split in enumerate(SPLITS):
+                    parts.append(sources[group][core][:, section * split : (section + 1) * split])
+    return jnp.concatenate(parts, axis=1)
 
 
 def project(length, x_ref, table_ref, vectors_ref, weight_ref, turned_ref, query_ref, key_ref, value_ref):
@@ -981,16 +945,13 @@
         attention.advance(0, every)
         weight_ref[core, ring.chip] = both_own[...]
         small_all[ring.chip] = small_own[...]
-        wide = stack_rows(gate_in[...], up_in[...]).astype(BF16)
+        wide = stack_rows(gate_in[...], up_in[...])
         for side in range(2):
             for group, span in enumerate(spans()):
-
-                def store(tile, part, side=side, first=group * spans()[0]):
-                    columns = slice(first + tile * LANES, first + (tile + 1) * LANES)
-                    perm_ref[side, 0, :, columns] = part[:rows].astype(BF16)
-                    perm_ref[side, 1, :, columns] = part[rows:].astype(BF16)
-
-                gather_columns(wide, side, group, store)
+                first = group * spans()[0]
+                part = gather_columns(wide, side, group).astype(BF16)
+                perm_ref[side, 0, :, first : first + span] = part[:rows]
+                perm_ref[side, 1, :, first : first + span] = part[rows:]
         trades[2].start()
         own = sum(SPLITS)
         for group, ref in enumerate((own_down1, own_down2)):
@@ -1442,15 +1403,24 @@
 
 def last_kernel(
     length,
-    d_query_ref, d_key_ref, d_value_ref, table_ref, turned_ref, x_ref, vectors_ref, weight_ref, d_hidden_ref,
-    output_grad_ref, second_ref, wide_first, down_first, wide_before, down_before, result_ref,
+    d_query_ref, d_key_ref, d_value_ref, table_ref, vectors_ref, output_grad_ref, second_ref,
+    wide_first, down_first, wide_before, down_before, result_ref, turned_in, x_in, weight_in, d_hidden_in,
     qkv_grad_out, output_grad_out, bits_out, gate_grad_out, up_grad_out, down_grad_out, input_grad_out, result_out,
     d_pre_ref, both_ref, part_ref, both_own, wide_own, down_own, bits_ref, bits_land, bits_sum,
-    input_grad_ref, input_grad_land, bits_send, bits_recv, swap_sems, bit_sems, *scratch,
+    input_grad_ref, input_grad_land, turned_ref, x_ref, weight_ref, d_hidden_ref,
+    bits_send, bits_recv, swap_sems, bit_sems, load_sems, *scratch,
 ):
     ring = Ring(CHIPS)
     core, mine = ring.core, ring.mine
     others = [{"fsdp": 2 * ring.chip_at(offset) + core} for offset in range(1, CHIPS)]
+    loads = [
+        pltpu.make_async_copy(src, dst, load_sems.at[k])
+        for k, (src, dst) in enumerate([
+            (turned_in, turned_ref), (weight_in, weight_ref), (x_in, x_ref), (d_hidden_in, d_hidden_ref),
+        ])
+    ]
+    for load in loads:
+        load.start()
     ring.greet(others + [ring.partner, ring.peer])
     share = Share(ring, wide_before, wide_own, scratch[:5])
     share_rows = ShareRows(ring, down_before, down_own, scratch[5:8])
@@ -1494,6 +1464,7 @@
         bias = part if bias is None else bias + part
 
     chip_rows = width // CHIPS
+    loads[0].wait()
     grad = mm(turned_ref[...], d_pre_ref[...]).astype(BF16)
     rest = grad.shape[1] - BOTH
     for chip in range(CHIPS):
@@ -1509,6 +1480,8 @@
     share_rows.second()
 
     gain = vectors_ref[1:2, :width]
+    for load in loads[1:]:
+        load.wait()
     weight_early, weight_late = weight_ref[0], weight_ref[1, :, : qwidth + 2 * LANES - BOTH]
     first = None
     for index in range(length // BLOCK):
@@ -1549,14 +1522,10 @@
     own_rows = gate_grad_out.shape[0]
     sources = []
     for ref in (wide_first, wide_own):
-        sources.append([stack_rows(ref[0, k], ref[1, k]).astype(BF16) for k in range(2)])
-
-    def store(tile, part):
-        columns = slice(tile * LANES, (tile + 1) * LANES)
-        gate_grad_out[:, columns] = part[:own_rows]
-        up_grad_out[:, columns] = part[own_rows:]
-
-    spread_columns(sources, store, gate_grad_out.shape[1])
+        sources.append([stack_rows(ref[0, k], ref[1, k]) for k in range(2)])
+    spread = spread_columns(sources)
+    gate_grad_out[...] = spread[:own_rows]
+    up_grad_out[...] = spread[own_rows:]
     share_both.first()
     total = bits_ref[ring.chip]
     for k, copy in enumerate(copies):
@@ -1590,9 +1559,9 @@
 ):
     tokens, width = d_hidden.shape
     ins = [
-        d_query, d_key, d_value, table, turned, x, vectors, weight, d_hidden, output_grad, second,
-        wide_first, down_first, wide_before, down_before,
+        d_query, d_key, d_value, table, vectors, output_grad, second, wide_first, down_first, wide_before, down_before,
     ]
+    far = [turned, x, weight, d_hidden]
     rows, span = wide_before.shape
     own_rows = rows // OWNERS
     own = sum(SPLITS)
@@ -1604,7 +1573,7 @@
     ]
     return pl.pallas_call(
         functools.partial(last_kernel, tokens),
-        in_specs=[pl.BlockSpec(memory_space=pltpu.VMEM)] * len(ins) + [ANY],
+        in_specs=[pl.BlockSpec(memory_space=pltpu.VMEM)] * len(ins) + [ANY] * 5,
         out_specs=[pl.BlockSpec(memory_space=pltpu.VMEM)] * len(outs) + [ANY],
         out_shape=[jax.ShapeDtypeStruct(shape, F32) for shape in outs]
         + [jax.ShapeDtypeStruct(result.shape, BF16)],
@@ -1614,8 +1583,9 @@
             pltpu.VMEM((2, 2, own_rows, span), F32), pltpu.VMEM((SPLITS[1], width), F32),
             pltpu.VMEM((CHIPS, BITS, LANES), F32), pltpu.VMEM((CHIPS - 1, BITS, LANES), F32),
             pltpu.VMEM((4, BITS, LANES), F32), pltpu.VMEM(halves, BF16), pltpu.VMEM(halves[1:], BF16),
-            dma(CHIPS - 1), dma(CHIPS - 1), dma(5), dma(4),
         ]
+        + [pltpu.VMEM(part.shape, part.dtype) for part in far]
+        + [dma(CHIPS - 1), dma(CHIPS - 1), dma(5), dma(4), dma(4)]
         + share_scratch(own_rows, span, True)
         + share_rows_scratch(SPLITS[1], width)
         + share_scratch(own_rows, BOTH, False)
@@ -1623,7 +1593,7 @@
         compiler_params=pltpu.CompilerParams(
             collective_id=3, has_side_effects=True, vmem_limit_bytes=VMEM_LIMIT
         ),
-    )(*ins, result)
+    )(*ins, result, *far)
 
 
 def ring_shards(

time: 428 us -> 426 us (level)
  no operation moved by 1% of the time
where the time goes in v2:
time: 426 us; the launch traced here: 423 us
  Pallas kernels  406 us (95%)
  local copies, waits for them, and re-layouts  11.7 us (3%)
  other arithmetic  4.73 us (1%)
    pallas_call x1, Pallas kernels, feed(): pl.pallas_call(functools.partial(feed_kernel, spread(3 * turns, HALVES, l...  161 us
    pallas_call x1, Pallas kernels, first_part(): pl.pallas_call(functools.partial(first_kernel, tokens, plan), grid=(PAIRS...  92.8 us
    pallas_call x1, Pallas kernels, back_all(): pl.pallas_call(functools.partial(back_kernel_all, tokens, plan), grid=(bl...  87.5 us
    pallas_call x1, Pallas kernels, last_part(): pl.pallas_call(functools.partial(last_kernel, tokens), in_specs=[pl.Block...  64.1 us
    unnamed x29, local copies, waits for them, and re-layouts  8.55 us

profile of v2, /device:TPU:0, one launch (start us, length us, event | category | flops | bytes accessed | tf_op | source)
XLA Modules:
  0.0 423.3 jit_solution(17730547820122109674)
XLA Ops:
  0.6 0.0 copy-start.5
  0.7 0.0 slice-start
  0.7 0.0 copy-start.7
  0.7 0.0 copy-start.10
  0.7 0.0 copy-start.9
  0.7 0.0 copy-start.8
  0.7 0.8 convert_element_type.15
  1.5 1.9 multiply_cosine_fusion
  3.4 1.3 pad_maximum_fusion.table_in
  4.7 0.0 copy-done.5
  4.7 0.0 slice-done
  4.7 0.0 copy-done.7
  4.7 0.7 pad_maximum_fusion.1.both_in
  5.4 0.0 copy-done.10
  5.4 0.0 copy-done.9
  5.5 0.0 copy-done.8
  5.5 0.1 copy.26
  5.6 0.6 pad.13.small_in
  6.2 92.8 %shard_map.186 = (bf16[2,512,896]{2,1,0:T(8,128)(2,1)}, f32[2,512,128]{2,1,0:T(8,128)}, bf16[2,8,112,1024]{3,2,1,0:T(8,128)(2,1)}, bf16[896,1024]{1,0:T(8,128)(2...) custom-call(bf16[2,512,896]{2,1,0:T(8,128)(2,1)} %x_in.1, ...), custom_call_target="tpu_custom_call" | custom-call | tf_op jit(solution)/shard_map/pallas_call | solution.py:1044
  99.1 161.4 %shard_map.187 = (f32[1024,896]{1,0:T(8,128)}, f32[1024,896]{1,0:T(8,128)}, bf16[2,1024,896]{2,1,0:T(8,128)(2,1)}, bf16[2,8,112,1408]{3,2,1,0:T(8,128)(2,1)}, bf...) custom-call(bf16[2,1024,896]{2,1,0:T(8,128)(2,1)} %get-tuple-element.55.normed_ref, ...), custom_call_target="tpu_custom_call" | custom-call | tf_op jit(solution)/shard_map/pallas_call | solution.py:1196
  260.4 87.5 %shard_map.188 = (f32[1024,896]{1,0:T(8,128)}, bf16[896,896]{1,0:T(8,128)(2,1)}, f32[1,896]{1,0:T(1,128)}, bf16[1024,896]{1,0:T(8,128)(2,1)}, f32[2,1024,128]{2,...) custom-call(f32[1024,896]{1,0:T(8,128)} %get-tuple-element.54.hidden, ...), custom_call_target="tpu_custom_call" | custom-call | tf_op jit(solution)/shard_map/pallas_call | solution.py:1383
  348.0 64.1 %shard_map.189 = (f32[28,1152]{1,0:T(8,128)}, f32[28,896]{1,0:T(8,128)}, f32[16,128]{1,0:T(8,128)}, f32[28,4864]{1,0:T(8,128)}, f32[28,4864]{1,0:T(8,128)}, /*in...) custom-call(bf16[1024,896]{1,0:T(8,128)(2,1)} %get-tuple-element.76.d_query_ref, ...), custom_call_target="tpu_custom_call" | custom-call | tf_op jit(solution)/shard_map/pallas_call | solution.py:1574
  412.1 0.0 copy-start
  412.1 0.8 constant_dynamic-slice_fusion
  413.0 0.5 slice_bitcast_fusion.1
  413.5 0.5 slice_bitcast_fusion.2
  414.0 0.5 slice_bitcast_fusion.3
  414.5 2.9 copy.34
  417.4 0.0 copy-done
  417.4 0.0 copy-start.4
  417.4 0.0 copy-start.6
  417.4 0.0 copy-start.2
  417.4 0.0 copy-start.1
  417.4 0.0 copy-start.3
  417.4 1.9 copy.35
  419.3 0.0 copy-done.4
  419.3 0.7 copy.36
  419.9 0.0 copy-done.6
  419.9 0.6 copy.37
  420.6 0.0 copy-done.2
  420.6 0.8 copy.38
  421.4 0.0 copy-done.1
  421.4 0.8 copy.39
  422.2 0.0 copy-done.3
  422.2 0.8 copy.40
  (4 shorter events, 0.0 us)
Async XLA Ops:
  0.6 4.1 copy-start.5
  0.7 4.0 slice-start
  0.7 4.0 copy-start.7
  0.7 4.8 %copy-start.10 = (bf16[56]{0:T(256)(128)(2,1)S(1)}, bf16[56]{0:T(256)(128)(2,1)}, u32[]{:S(2)}) copy-start(bf16[56]{0:T(256)(128)(2,1)} %param.16) | copy-start | bytes 340
  0.7 4.8 %copy-start.9 = (bf16[56]{0:T(256)(128)(2,1)S(1)}, bf16[56]{0:T(256)(128)(2,1)}, u32[]{:S(2)}) copy-start(bf16[56]{0:T(256)(128)(2,1)} %param.20) | copy-start | bytes 340
  0.7 4.8 %copy-start.8 = (bf16[72]{0:T(256)(128)(2,1)S(1)}, bf16[72]{0:T(256)(128)(2,1)}, u32[]{:S(2)}) copy-start(bf16[72]{0:T(256)(128)(2,1)} %param.14) | copy-start | bytes 436
  412.1 5.3 %copy-start = (f32[2,512,896]{2,1,0:T(8,128)S(1)}, f32[2,512,896]{2,1,0:T(8,128)}, u32[]{:S(2)}) copy-start(f32[2,512,896]{2,1,0:T(8,128)} %get-tuple-element.119) | copy-start | bytes 11010052
  417.4 1.9 copy-start.4
  417.4 2.6 copy-start.6
  417.4 3.2 copy-start.2
  417.4 4.0 copy-start.1
  417.4 4.9 %copy-start.3 = (f32[152,896]{1,0:T(8,128)S(1)}, f32[152,896]{1,0:T(8,128)}, u32[]{:S(2)}) copy-start(f32[152,896]{1,0:T(8,128)} %get-tuple-element.126) | copy-start | bytes 1634308

commit v3 on v2

--- a/solution.py
+++ b/solution.py
@@ -1378,7 +1378,7 @@
     ]
     moves = [(hop, half) for hop in range(CHIPS) for half in HALVES]
     plan = [[] for _ in range(2 * (blocks + PAIRS) + 1)]
-    for place, move in zip([2 * blocks - 4, 2 * blocks - 2] + list(range(2 * blocks, len(plan) - 1)), moves):
+    for place, move in zip([2, 4, 6] + list(range(2 * blocks, len(plan) - 2)), moves):
         plan[place].append(move)
     return pl.pallas_call(
         functools.partial(back_kernel_all, tokens, plan),
@@ -1441,6 +1441,8 @@
     share_rows.first()
     result_keep = pltpu.make_async_copy(result_ref.at[mine], result_out.at[mine], swap_sems.at[4])
     result_swap = remote(result_ref.at[1 - mine], result_out.at[mine], swap_sems.at[2], swap_sems.at[3], ring.peer)
+    result_keep.start()
+    result_swap.start()
 
     qwidth = HEADS * HEAD_DIM
     width = d_hidden_ref.shape[1]
@@ -1474,8 +1476,6 @@
         both_ref[1, chip, :, rest:] = output_grad_ref[rows, :]
     reduce.begin()
     reduce.advance(0, range(len(pieces)))
-    result_keep.start()
-    result_swap.start()
     share.second()
     share_rows.second()
 

time: 426 us -> 429 us (level)
  no operation moved by 1% of the time
where the time goes in v3:
time: 429 us; the launch traced here: 427 us
  Pallas kernels  409 us (95%)
  local copies, waits for them, and re-layouts  11.7 us (3%)
  other arithmetic  4.73 us (1%)
    pallas_call x1, Pallas kernels, feed(): pl.pallas_call(functools.partial(feed_kernel, spread(3 * turns, HALVES, l...  161 us
    pallas_call x1, Pallas kernels, first_part(): pl.pallas_call(functools.partial(first_kernel, tokens, plan), grid=(PAIRS...  92.8 us
    pallas_call x1, Pallas kernels, back_all(): pl.pallas_call(functools.partial(back_kernel_all, tokens, plan), grid=(bl...  90.8 us
    pallas_call x1, Pallas kernels, last_part(): pl.pallas_call(functools.partial(last_kernel, tokens), in_specs=[pl.Block...  64.1 us

profile of v3, /device:TPU:0, one launch (start us, length us, event | category | flops | bytes accessed | tf_op | source)
XLA Modules:
  0.0 426.5 jit_solution(3170773424593941496)
XLA Ops:
  0.6 0.0 copy-start.5
  0.7 0.0 slice-start
  0.7 0.0 copy-start.7
  0.7 0.0 copy-start.10
  0.7 0.0 copy-start.9
  0.7 0.0 copy-start.8
  0.7 0.8 convert_element_type.15
  1.5 1.9 multiply_cosine_fusion
  3.4 1.3 pad_maximum_fusion.table_in
  4.7 0.0 copy-done.5
  4.7 0.0 slice-done
  4.7 0.0 copy-done.7
  4.7 0.7 pad_maximum_fusion.1.both_in
  5.4 0.0 copy-done.10
  5.4 0.0 copy-done.9
  5.5 0.0 copy-done.8
  5.5 0.1 copy.26
  5.6 0.6 pad.13.small_in
  6.2 92.8 %shard_map.186 = (bf16[2,512,896]{2,1,0:T(8,128)(2,1)}, f32[2,512,128]{2,1,0:T(8,128)}, bf16[2,8,112,1024]{3,2,1,0:T(8,128)(2,1)}, bf16[896,1024]{1,0:T(8,128)(2...) custom-call(bf16[2,512,896]{2,1,0:T(8,128)(2,1)} %x_in.1, ...), custom_call_target="tpu_custom_call" | custom-call | tf_op jit(solution)/shard_map/pallas_call | solution.py:1044
  99.1 161.4 %shard_map.187 = (f32[1024,896]{1,0:T(8,128)}, f32[1024,896]{1,0:T(8,128)}, bf16[2,1024,896]{2,1,0:T(8,128)(2,1)}, bf16[2,8,112,1408]{3,2,1,0:T(8,128)(2,1)}, bf...) custom-call(bf16[2,1024,896]{2,1,0:T(8,128)(2,1)} %get-tuple-element.55.normed_ref, ...), custom_call_target="tpu_custom_call" | custom-call | tf_op jit(solution)/shard_map/pallas_call | solution.py:1196
  260.4 90.8 %shard_map.188 = (f32[1024,896]{1,0:T(8,128)}, bf16[896,896]{1,0:T(8,128)(2,1)}, f32[1,896]{1,0:T(1,128)}, bf16[1024,896]{1,0:T(8,128)(2,1)}, f32[2,1024,128]{2,...) custom-call(f32[1024,896]{1,0:T(8,128)} %get-tuple-element.54.hidden, ...), custom_call_target="tpu_custom_call" | custom-call | tf_op jit(solution)/shard_map/pallas_call | solution.py:1383
  351.3 64.1 %shard_map.189 = (f32[28,1152]{1,0:T(8,128)}, f32[28,896]{1,0:T(8,128)}, f32[16,128]{1,0:T(8,128)}, f32[28,4864]{1,0:T(8,128)}, f32[28,4864]{1,0:T(8,128)}, /*in...) custom-call(bf16[1024,896]{1,0:T(8,128)(2,1)} %get-tuple-element.76.d_query_ref, ...), custom_call_target="tpu_custom_call" | custom-call | tf_op jit(solution)/shard_map/pallas_call | solution.py:1574
  415.3 0.0 copy-start
  415.4 0.8 constant_dynamic-slice_fusion
  416.2 0.5 slice_bitcast_fusion.1
  416.7 0.5 slice_bitcast_fusion.2
  417.2 0.5 slice_bitcast_fusion.3
  417.7 2.9 copy.34
  420.6 0.0 copy-done
  420.6 0.0 copy-start.4
  420.6 0.0 copy-start.6
  420.6 0.0 copy-start.2
  420.6 0.0 copy-start.1
  420.6 0.0 copy-start.3
  420.6 1.9 copy.35
  422.5 0.0 copy-done.4
  422.5 0.7 copy.36
  423.2 0.0 copy-done.6
  423.2 0.6 copy.37
  423.8 0.0 copy-done.2
  423.8 0.8 copy.38
  424.7 0.0 copy-done.1
  424.7 0.8 copy.39
  425.5 0.0 copy-done.3
  425.5 0.8 copy.40
  (4 shorter events, 0.0 us)
Async XLA Ops:
  0.6 4.1 copy-start.5
  0.7 4.0 slice-start
  0.7 4.0 copy-start.7
  0.7 4.8 %copy-start.10 = (bf16[56]{0:T(256)(128)(2,1)S(1)}, bf16[56]{0:T(256)(128)(2,1)}, u32[]{:S(2)}) copy-start(bf16[56]{0:T(256)(128)(2,1)} %param.16) | copy-start | bytes 340
  0.7 4.8 %copy-start.9 = (bf16[56]{0:T(256)(128)(2,1)S(1)}, bf16[56]{0:T(256)(128)(2,1)}, u32[]{:S(2)}) copy-start(bf16[56]{0:T(256)(128)(2,1)} %param.20) | copy-start | bytes 340
  0.7 4.8 %copy-start.8 = (bf16[72]{0:T(256)(128)(2,1)S(1)}, bf16[72]{0:T(256)(128)(2,1)}, u32[]{:S(2)}) copy-start(bf16[72]{0:T(256)(128)(2,1)} %param.14) | copy-start | bytes 436
  415.3 5.3 %copy-start = (f32[2,512,896]{2,1,0:T(8,128)S(1)}, f32[2,512,896]{2,1,0:T(8,128)}, u32[]{:S(2)}) copy-start(f32[2,512,896]{2,1,0:T(8,128)} %get-tuple-element.119) | copy-start | bytes 11010052
  420.6 1.9 copy-start.4
  420.6 2.6 copy-start.6
  420.6 3.2 copy-start.2
  420.6 4.0 copy-start.1
  420.6 4.9 %copy-start.3 = (f32[152,896]{1,0:T(8,128)S(1)}, f32[152,896]{1,0:T(8,128)}, u32[]{:S(2)}) copy-start(f32[152,896]{1,0:T(8,128)} %get-tuple-element.126) | copy-start | bytes 1634308
